TPU v7x, 32 devices: a whole 2x2x4 slice. The times are simulated.
32 devices in a mesh: groups: 2 (over x), vel: 16 (over z, y, core).
Axes of the slice: x: 2, y: 2, z: 4, core: 2. Of those that a mesh axis runs over, the one named last changes fastest.
Arguments:
- epoch_maps: bfloat16 [128, 192, 512], P('vel', 'groups'), parts along dimension 1, may hold values from -6 to 6, as said below
- velocity: int32 [16, 2], P('vel'), may hold values from -16 to 16, as said below
- slot_epoch: int32 [64], replicated, may hold values from 0 to 63, each once
- epoch_time: int32 [64], replicated, may hold values from 0 to 127, as said below
Outputs:
- likelihood: float32 [16, 192, 512], P('vel', 'groups'), parts along dimension 1
- best_value: float32 [192, 512], P('groups'), parts along dimension 0
There are 2 independent parts, one for each index of `groups`. A program takes and returns all parts, laid end to end along the dimension named above; an argument that names none is the same for every part. Nothing has to cross between parts.
Inputs may be any that keep to these rules, and one draw needn't show every extreme that they name: `epoch_maps`: the first 64 images are likelihoods, the others weights of at least 0.25 and at most 4. `velocity`: all rows are distinct; rows (16, 16) and (-16, -16) both occur. `epoch_time`: strictly increasing, the first 0 and the last 127. `slot_epoch`: each epoch stands in exactly one slot.
All inputs are finite; a program needn't handle non-finite values.
Results may differ from a plain program's by a relative error of at most 0.0029.
Values may be sent and summed in bfloat16 or wider, within the bound.
No kernel may reach another device: no remote copies, remote signals or barrier semaphores. Data moves between devices by JAX's collectives and lax.ppermute only.
A program may use at most 64 MiB of HBM per device.

v0:
```python
import math

import jax
import jax.numpy as jnp
import numpy as np
from jax import lax
from jax.sharding import PartitionSpec as P

SPLINE = np.array(
    [
        [64.0, 256.0, 64.0, 0.0],
        [27.0, 235.0, 121.0, 1.0],
        [8.0, 184.0, 184.0, 8.0],
        [1.0, 121.0, 235.0, 27.0],
    ],
    np.float32,
)
spline_norm = 147456.0
rate_divisor = 32


def spline_taps(offset):
    whole_shift = offset // 4
    fraction = offset - 4 * whole_shift
    weights = []
    for tap_number in range(4):
        tap_value = jnp.zeros(offset.shape, jnp.float32)
        for fraction_level in range(4):
            tap_value = tap_value + jnp.where(
                fraction == fraction_level, float(SPLINE[fraction_level, tap_number]), 0.0
            )
        weights.append(tap_value)
    return (whole_shift, weights)


def band_matrix(whole_shift, weights, length):
    outputs = lax.broadcasted_iota(jnp.int32, (length, length), 0)
    inputs = lax.broadcasted_iota(jnp.int32, (length, length), 1)
    distance = inputs[None, None] - outputs[None, None] - whole_shift[:, :, None, None] + 1
    matrix = jnp.zeros(distance.shape, jnp.float32)
    for tap_number in range(4):
        matrix = matrix + jnp.where(
            distance == tap_number, weights[tap_number][:, :, None, None], 0.0
        )
    return matrix.astype(jnp.bfloat16)


def lookup_times(slot_ids, slot_time):
    epochs = slot_time.shape[0]
    table = (
        slot_ids[:, None] == lax.broadcasted_iota(jnp.int32, (slot_ids.shape[0], epochs), 1)
    ).astype(jnp.int32)
    return jnp.sum(table * slot_time[None, :], axis=1)


def shift_bands(times, rate_rows, rows_length, columns_length):
    row_whole, row_weights = spline_taps(times[:, None] * rate_rows[None, :, 0] // rate_divisor)
    column_whole, column_weights = spline_taps(
        times[:, None] * rate_rows[None, :, 1] // rate_divisor
    )
    return (
        band_matrix(row_whole, row_weights, rows_length),
        band_matrix(column_whole, column_weights, columns_length),
    )


def local(epoch_maps, velocity, slot_epoch, epoch_time):
    epochs = slot_epoch.shape[0]
    slot_time = lookup_times(slot_epoch, epoch_time)
    rows_length = epoch_maps.shape[1]
    columns_length = epoch_maps.shape[2]
    local_velocities = velocity.shape[0]
    initial = jnp.zeros((local_velocities, 2, rows_length, columns_length), jnp.float32)
    gathered = lax.all_gather(epoch_maps, "vel", axis=0, tiled=True)
    paired = gathered.reshape(2, epochs, rows_length, columns_length)
    block_size = math.gcd(epochs, 8)

    def one_block(block_index, running):
        block_first = block_index * block_size
        images = lax.dynamic_slice_in_dim(paired, block_first, block_size, 1)
        block_times = lax.dynamic_slice_in_dim(slot_time, block_first, block_size, 0)
        row_band, column_band = shift_bands(block_times, velocity, rows_length, columns_length)
        rows_done = jnp.einsum(
            "pvoi,mpij->pvmoj", row_band, images, preferred_element_type=jnp.float32
        ).astype(jnp.bfloat16)
        return running + jnp.einsum(
            "pvmoj,pvcj->vmoc", rows_done, column_band, preferred_element_type=jnp.float32
        )

    totals = lax.fori_loop(0, epochs // block_size, one_block, initial)
    stack_sums = totals / spline_norm
    likelihood = stack_sums[:, 0] / jnp.sqrt(stack_sums[:, 1] + 1.0)
    best_value = lax.pmax(jnp.max(likelihood, axis=0), "vel")
    return (likelihood, best_value)


def solution(mesh):
    return jax.shard_map(
        local,
        mesh=mesh,
        in_specs=(P("vel", "groups", None), P("vel", None), P(), P()),
        out_specs=(P("vel", "groups", None), P("groups", None)),
        check_vma=False,
    )
```

profile of v0, /device:TPU:0, one launch (start us, length us, event | category | flops | bytes accessed | tf_op | source)
XLA Modules:
  0.0 283.1 jit_solution(15816745322282400095)
XLA Ops:
  7.2 0.0 all-gather.2.cloned.1.call-start
  7.2 0.7 all-gather.2.cloned.1.call-update
  7.9 0.0 all-reduce.2.cloned.1.call-start
  8.0 0.8 select_reduce_fusion
  8.8 105.0 %all-gather.2.cloned.1.call-done = bf16[128,96,512]{2,1,0:T(8,128)(2,1)} async-done(((bf16[8,96,512]{2,1,0:T(8,128)(2,1)}), bf16[128,96,512]{2,1,0:T(8,128)(2,1)}) %all-gather.2.cloned.1.call-update) | async-done | bytes 12582928 | tf_op jit(solution)/shard_map/all_gather | solution.py:74
  113.8 71.9 %while.17 = (s32[]{:T(128)}, f32[1,2,96,512]{3,2,1,0:T(8,128)S(1)}, bf16[2,64,96,512]{3,2,1,0:T(8,128)(2,1)}, s32[64]{0:T(128)S(1)}, s32[1,2]{1,0:T(1,128)}, /*index=5*/s32[]{:T(128)}, s32[]{:T(128)}, s32[]{:T(128)}, s32[]{:T(128)}) while((s32[]{:T(128)}, f32[1,2,96,512]{3,2,1,0:T(8,128)S(1)}, bf16[2,64,96,512]{3,2,1,0:T(8,128)(2,1)}, ...), condition=%wide.region_2.3_spmd.clone, body=%wide.region_1.2_spmd.clone.sunk | while | flops 987949120 | bytes 4531293 | solution.py:90
  113.8 1.3 fusion.85
  115.1 1.4 and_select_fusion.7
  116.5 0.1 iota_subtract_fusion.4
  116.7 6.1 %fusion.86 = f32[1,2,96,512]{3,2,1,0:T(8,128)S(1)} fusion(f32[8]{0:T(128)S(1)} %get-tuple-element.275, f32[8]{0:T(128)S(1)} %get-tuple-element.276, f32[8]{0:T(128)S(1)} %get-tuple-element.277, f32[8]{0:T(128)S(1)} %get-tuple-element.278, s32[8]{0:T(128)S(1)} %get-tuple-element.279, s32[512,512]{1,0:T(8,128)S(1)} %iota_subtract_fusion.4, ...), kind=kOutput, calls=%fused_computation.12.clone.1 | convolution fusion | flops 987676672 | bytes 3445061 | tf_op jit(solution)/shard_map/while/body/eval_jaxpr/pvmoj,pvcj->vmoc/dot_general | solution.py:86
  122.8 1.3 fusion.85
  124.1 1.4 and_select_fusion.7
  125.5 0.1 iota_subtract_fusion.4
  125.7 6.1 %fusion.86 = f32[1,2,96,512]{3,2,1,0:T(8,128)S(1)} fusion(f32[8]{0:T(128)S(1)} %get-tuple-element.275, f32[8]{0:T(128)S(1)} %get-tuple-element.276, f32[8]{0:T(128)S(1)} %get-tuple-element.277, f32[8]{0:T(128)S(1)} %get-tuple-element.278, s32[8]{0:T(128)S(1)} %get-tuple-element.279, s32[512,512]{1,0:T(8,128)S(1)} %iota_subtract_fusion.4, ...), kind=kOutput, calls=%fused_computation.12.clone.1 | convolution fusion | flops 987676672 | bytes 3445061 | tf_op jit(solution)/shard_map/while/body/eval_jaxpr/pvmoj,pvcj->vmoc/dot_general | solution.py:86
  131.7 1.3 fusion.85
  133.1 1.4 and_select_fusion.7
  134.5 0.1 iota_subtract_fusion.4
  134.6 6.1 %fusion.86 = f32[1,2,96,512]{3,2,1,0:T(8,128)S(1)} fusion(f32[8]{0:T(128)S(1)} %get-tuple-element.275, f32[8]{0:T(128)S(1)} %get-tuple-element.276, f32[8]{0:T(128)S(1)} %get-tuple-element.277, f32[8]{0:T(128)S(1)} %get-tuple-element.278, s32[8]{0:T(128)S(1)} %get-tuple-element.279, s32[512,512]{1,0:T(8,128)S(1)} %iota_subtract_fusion.4, ...), kind=kOutput, calls=%fused_computation.12.clone.1 | convolution fusion | flops 987676672 | bytes 3445061 | tf_op jit(solution)/shard_map/while/body/eval_jaxpr/pvmoj,pvcj->vmoc/dot_general | solution.py:86
  140.7 1.3 fusion.85
  142.1 1.4 and_select_fusion.7
  143.5 0.1 iota_subtract_fusion.4
  143.6 6.1 %fusion.86 = f32[1,2,96,512]{3,2,1,0:T(8,128)S(1)} fusion(f32[8]{0:T(128)S(1)} %get-tuple-element.275, f32[8]{0:T(128)S(1)} %get-tuple-element.276, f32[8]{0:T(128)S(1)} %get-tuple-element.277, f32[8]{0:T(128)S(1)} %get-tuple-element.278, s32[8]{0:T(128)S(1)} %get-tuple-element.279, s32[512,512]{1,0:T(8,128)S(1)} %iota_subtract_fusion.4, ...), kind=kOutput, calls=%fused_computation.12.clone.1 | convolution fusion | flops 987676672 | bytes 3445061 | tf_op jit(solution)/shard_map/while/body/eval_jaxpr/pvmoj,pvcj->vmoc/dot_general | solution.py:86
  149.7 1.3 fusion.85
  151.1 1.4 and_select_fusion.7
  152.5 0.1 iota_subtract_fusion.4
  152.6 6.1 %fusion.86 = f32[1,2,96,512]{3,2,1,0:T(8,128)S(1)} fusion(f32[8]{0:T(128)S(1)} %get-tuple-element.275, f32[8]{0:T(128)S(1)} %get-tuple-element.276, f32[8]{0:T(128)S(1)} %get-tuple-element.277, f32[8]{0:T(128)S(1)} %get-tuple-element.278, s32[8]{0:T(128)S(1)} %get-tuple-element.279, s32[512,512]{1,0:T(8,128)S(1)} %iota_subtract_fusion.4, ...), kind=kOutput, calls=%fused_computation.12.clone.1 | convolution fusion | flops 987676672 | bytes 3445061 | tf_op jit(solution)/shard_map/while/body/eval_jaxpr/pvmoj,pvcj->vmoc/dot_general | solution.py:86
  158.7 1.3 fusion.85
  160.0 1.4 and_select_fusion.7
  161.5 0.1 iota_subtract_fusion.4
  161.6 6.1 %fusion.86 = f32[1,2,96,512]{3,2,1,0:T(8,128)S(1)} fusion(f32[8]{0:T(128)S(1)} %get-tuple-element.275, f32[8]{0:T(128)S(1)} %get-tuple-element.276, f32[8]{0:T(128)S(1)} %get-tuple-element.277, f32[8]{0:T(128)S(1)} %get-tuple-element.278, s32[8]{0:T(128)S(1)} %get-tuple-element.279, s32[512,512]{1,0:T(8,128)S(1)} %iota_subtract_fusion.4, ...), kind=kOutput, calls=%fused_computation.12.clone.1 | convolution fusion | flops 987676672 | bytes 3445061 | tf_op jit(solution)/shard_map/while/body/eval_jaxpr/pvmoj,pvcj->vmoc/dot_general | solution.py:86
  167.7 1.3 fusion.85
  169.0 1.4 and_select_fusion.7
  170.5 0.1 iota_subtract_fusion.4
  170.6 6.1 %fusion.86 = f32[1,2,96,512]{3,2,1,0:T(8,128)S(1)} fusion(f32[8]{0:T(128)S(1)} %get-tuple-element.275, f32[8]{0:T(128)S(1)} %get-tuple-element.276, f32[8]{0:T(128)S(1)} %get-tuple-element.277, f32[8]{0:T(128)S(1)} %get-tuple-element.278, s32[8]{0:T(128)S(1)} %get-tuple-element.279, s32[512,512]{1,0:T(8,128)S(1)} %iota_subtract_fusion.4, ...), kind=kOutput, calls=%fused_computation.12.clone.1 | convolution fusion | flops 987676672 | bytes 3445061 | tf_op jit(solution)/shard_map/while/body/eval_jaxpr/pvmoj,pvcj->vmoc/dot_general | solution.py:86
  176.7 1.3 fusion.85
  178.0 1.4 and_select_fusion.7
  179.4 0.1 iota_subtract_fusion.4
  179.6 6.1 %fusion.86 = f32[1,2,96,512]{3,2,1,0:T(8,128)S(1)} fusion(f32[8]{0:T(128)S(1)} %get-tuple-element.275, f32[8]{0:T(128)S(1)} %get-tuple-element.276, f32[8]{0:T(128)S(1)} %get-tuple-element.277, f32[8]{0:T(128)S(1)} %get-tuple-element.278, s32[8]{0:T(128)S(1)} %get-tuple-element.279, s32[512,512]{1,0:T(8,128)S(1)} %iota_subtract_fusion.4, ...), kind=kOutput, calls=%fused_computation.12.clone.1 | convolution fusion | flops 987676672 | bytes 3445061 | tf_op jit(solution)/shard_map/while/body/eval_jaxpr/pvmoj,pvcj->vmoc/dot_general | solution.py:86
  185.7 0.8 fusion.72
  186.5 0.0 all-reduce.2.cloned.1.call-update
  186.5 88.1 %all-reduce.2.cloned.1.call-done = f32[96,512]{1,0:T(8,128)} async-done(((f32[96,512]{1,0:T(8,128)}), f32[96,512]{1,0:T(8,128)}) %all-reduce.2.cloned.1.call-update) | async-done | bytes 196624 | tf_op jit(solution)/shard_map/pmax | solution.py:93
  274.6 1.6 copy.33
  (34 shorter events, 0.4 us)
Async XLA Ops:
  7.2 106.6 %all-gather.2.cloned.1.call-start = ((), (), s32[]{:S(2)}) async-start(), calls=%async_computation | async-start | bytes 13369344 | tf_op jit(solution)/shard_map/all_gather | solution.py:74
  7.9 266.7 %all-reduce.2.cloned.1.call-start = ((), (), s32[]{:S(2)}) async-start(), calls=%async_computation.1 | async-start | bytes 393216 | tf_op jit(solution)/shard_map/pmax | solution.py:93
Sparse Core Ops, SparseCore 0:
  10.3 103.4 all-gather.1
  186.6 87.9 all-reduce.1
where the time goes:
time: 284 us; the launch traced here: 283 us
  waiting for transfers between devices  194 us (68%)
  matrix products  48.5 us (17%)
  between operations  14.1 us (5%)
  other arithmetic  13.9 us (5%)
  local copies, waits for them, and re-layouts  12.3 us (4%)
    all_gather x1, waiting for transfers between devices, local(): gathered = lax.all_gather(epoch_maps, 'vel', axis=0, tiled=True)  105 us
    pmax x1, waiting for transfers between devices, local(): best_value = lax.pmax(jnp.max(likelihood, axis=0), 'vel')  88.1 us
    dot_general x8, matrix products, one_block(): jnp.einsum('pvmoj,pvcj->vmoc', rows_done, column_band, preferred_element_...  48.5 us
    select_n x8, other arithmetic, shift_bands(): times[:, None] * rate_rows[None, :, 0] // rate_divisor  10.9 us
    slice x8, local copies, waits for them, and re-layouts, shift_bands(): rate_rows[None, :, 0]  10.7 us
  transfers between devices with their start and end apart: 2, of which 2 were waited for; matrix products, arithmetic and copies ran while one was open for 0% of the time, Pallas kernels for 0%

commit v1 on v0

v1 whole, which is shorter than its diff:
```python
import functools

import jax
import jax.numpy as jnp
import ml_dtypes
import numpy as np
from jax import lax
from jax.experimental import pallas as pl
from jax.experimental.pallas import tpu as pltpu
from jax.sharding import PartitionSpec as P

SPLINE = np.array(
    [
        [64.0, 256.0, 64.0, 0.0],
        [27.0, 235.0, 121.0, 1.0],
        [8.0, 184.0, 184.0, 8.0],
        [1.0, 121.0, 235.0, 27.0],
    ],
    np.float32,
)
spline_norm = 147456.0
rate_divisor = 32
REACH = 16
HALO = 32
LANES = 128
LINK_SCALE = 64.0


def row_filters(rows, lanes):
    offsets = sorted({(rows * j) % LANES for j in range(max(1, lanes // rows))})
    bands = np.zeros((len(offsets), 2 * LANES, 4 * LANES), np.float32)
    for number, offset in enumerate(offsets):
        for row in range(rows):
            for tap in range(4):
                for fraction in range(4):
                    place = (row - tap + 1) % LANES
                    bands[number, offset + row, fraction * LANES + place] = SPLINE[fraction, tap]
    return offsets, bands.astype(ml_dtypes.bfloat16)


def window_kernel(block, chips, place_ref, image_ref, *refs):
    *window_refs, padded = refs
    columns = image_ref.shape[1]
    padded[:HALO] = jnp.zeros((HALO, padded.shape[1]), padded.dtype)
    padded[HALO + columns :] = jnp.zeros((HALO, padded.shape[1]), padded.dtype)
    for first in range(0, columns, LANES):
        padded[HALO + first : HALO + first + LANES] = image_ref[:, first : first + LANES].T
    for relative, window_ref in enumerate(window_refs):
        chip = place_ref[0] ^ relative
        start = pl.multiple_of(chip * block, block)
        window_ref[...] = padded[pl.ds(start, block + 2 * HALO)]


def stack_kernel(
    block, rows, per_device, epochs, offsets, device_ref, velocity_ref, slot_ref, time_ref, filter_ref, *refs
):
    *window_refs, out_ref, filtered, bins = refs
    hypotheses = velocity_ref.shape[0]
    tall = bins.shape[1]
    bins[...] = jnp.zeros(bins.shape, bins.dtype)
    for relative, window_ref in enumerate(window_refs):
        source = device_ref[0] ^ (2 * relative)
        lanes = window_ref.shape[1]
        for number in range(per_device):
            slot = lax.rem(source * per_device + number, epochs)
            time = time_ref[slot_ref[slot]]
            low = rows * number // LANES * LANES
            high = min(lanes, (rows * (number + 1) + LANES - 1) // LANES * LANES)
            band = filter_ref[offsets.index(rows * number - low), : high - low, :]
            product = jnp.dot(window_ref[:, low:high], band, preferred_element_type=jnp.float32)
            product = product.astype(jnp.bfloat16).astype(jnp.float32)
            for fraction in range(4):
                filtered[fraction] = product[:, fraction * LANES : (fraction + 1) * LANES]

            @pl.loop(0, hypotheses, unroll=min(hypotheses, 16))
            def add(v):
                row_offset = (velocity_ref[v, 0] * time) >> 5
                column_offset = (velocity_ref[v, 1] * time) >> 5
                start = HALO - 1 + (column_offset >> 2)
                shifted = filtered[row_offset & 3, pl.ds(start, tall), :]
                shifted = pltpu.roll(shifted, (LANES - (row_offset >> 2)) & (LANES - 1), 1)
                place = 4 * v + (column_offset & 3)
                bins[place] = bins[place] + shifted

    @pl.loop(0, hypotheses)
    def finish(v):
        total = jnp.zeros((block, LANES), jnp.float32)
        for fraction in range(4):
            for tap in range(4):
                if SPLINE[fraction, tap]:
                    total = total + float(SPLINE[fraction, tap]) * bins[4 * v + fraction, tap : tap + block, :]
        out_ref[v & 1, v >> 1] = (total * (1.0 / spline_norm)).T[:rows]


def assemble_kernel(block, place_ref, *refs):
    *piece_refs, likelihood_ref, best_ref = refs
    for relative, piece_ref in enumerate(piece_refs):
        chip = place_ref[0] ^ relative
        for c in range(len(piece_refs)):

            @pl.when(chip == c)
            def put():
                likelihood_ref[0, :, c * block : (c + 1) * block] = piece_ref[0]
                best_ref[:, c * block : (c + 1) * block] = piece_ref[1]


def local(axis_size, epoch_maps, velocity, slot_epoch, epoch_time):
    per_device, rows, columns = epoch_maps.shape
    epochs = slot_epoch.shape[0]
    half = axis_size // 2
    chips = half // 2
    block = columns // chips
    device = lax.axis_index("vel").astype(jnp.int32)
    place = (device % half // 2).reshape(1)

    def swap(array, bits):
        return lax.ppermute(array, "vel", [(i, i ^ bits) for i in range(axis_size)])

    smem = pl.BlockSpec(memory_space=pltpu.SMEM)
    vmem = pl.BlockSpec(memory_space=pltpu.VMEM)
    lanes = per_device * rows
    wide = block + 2 * HALO
    windows = pl.pallas_call(
        functools.partial(window_kernel, block, chips),
        out_shape=[jax.ShapeDtypeStruct((wide, lanes), epoch_maps.dtype)] * chips,
        in_specs=[smem, vmem],
        out_specs=[vmem] * chips,
        scratch_shapes=[pltpu.VMEM((columns + 2 * HALO, lanes), epoch_maps.dtype)],
        name="windows",
    )(place, epoch_maps.reshape(lanes, columns))
    windows = [windows[0]] + [swap(windows[x], 2 * x) for x in range(1, chips)]

    rates = jnp.concatenate([velocity, swap(velocity, 1)])
    rates = jnp.concatenate([rates] + [swap(rates, 2 * x) for x in range(1, chips)])
    rates = jnp.concatenate([rates, swap(rates, half)])

    offsets, bands = row_filters(rows, lanes)
    tall = (block + 3 + 7) // 8 * 8
    partial = pl.pallas_call(
        functools.partial(stack_kernel, block, rows, per_device, epochs, offsets),
        out_shape=jax.ShapeDtypeStruct((2, half, rows, block), jnp.float32),
        in_specs=[smem] * 4 + [vmem] * (1 + chips),
        out_specs=vmem,
        scratch_shapes=[
            pltpu.VMEM((4, wide, LANES), jnp.float32),
            pltpu.VMEM((4 * axis_size, tall, LANES), jnp.float32),
        ],
        compiler_params=pltpu.CompilerParams(vmem_limit_bytes=48 * 1024 * 1024),
        name="stack",
    )(device.reshape(1), rates, slot_epoch, epoch_time, jnp.asarray(bands), *windows)

    own = ((partial[0] + swap(partial[1], 1)) * LINK_SCALE).astype(jnp.float16)
    other = swap(own, half)
    other = jnp.concatenate([other[chips:], other[:chips]])
    own = own.astype(jnp.float32) * (1.0 / LINK_SCALE)
    other = other.astype(jnp.float32) * (1.0 / LINK_SCALE)
    first = device < half
    sums = jnp.where(first, own, other)
    weights = jnp.where(first, other, own)
    likelihood = sums / jnp.sqrt(weights + 1.0)
    best = jnp.max(likelihood, axis=0)
    best = jnp.maximum(best, swap(best, 1))
    pieces = [jnp.stack([likelihood[x], best]) for x in range(chips)]
    pieces = [pieces[0]] + [swap(pieces[x], 2 * x) for x in range(1, chips)]
    return pl.pallas_call(
        functools.partial(assemble_kernel, block),
        out_shape=[
            jax.ShapeDtypeStruct((1, rows, columns), jnp.float32),
            jax.ShapeDtypeStruct((rows, columns), jnp.float32),
        ],
        in_specs=[smem] + [vmem] * chips,
        out_specs=[vmem] * 2,
        name="assemble",
    )(place, *pieces)


def solution(mesh):
    return jax.shard_map(
        functools.partial(local, mesh.shape["vel"]),
        mesh=mesh,
        in_specs=(P("vel", "groups", None), P("vel", None), P(), P()),
        out_specs=(P("vel", "groups", None), P("groups", None)),
        check_vma=False,
    )
```

time: 284 us -> 71.7 us (0.25)
  waiting for transfers between devices: 194 us -> 25.8 us
  matrix products: 48.5 us -> 0 us
  Pallas kernels: 0 us -> 20.2 us
  starting transfers between devices: 0.08 us -> 20.1 us
  between operations: 14.1 us -> 0.76 us
  other arithmetic: 13.9 us -> 0.89 us
  local copies, waits for them, and re-layouts: 12.3 us -> 3.62 us
    all_gather x1 -> x0, waiting for transfers between devices: 105 us -> none  [local(): gathered = lax.all_gather(epoch_maps, 'vel', axis=0, tiled=True)]
    pmax x1 -> x0, waiting for transfers between devices: 88.1 us -> none  [local(): best_value = lax.pmax(jnp.max(likelihood, axis=0), 'vel')]
    dot_general x8 -> x0, matrix products: 48.5 us -> none  [one_block(): jnp.einsum('pvmoj,pvcj->vmoc', rows_done, column_band, preferred_element_...]
    ppermute x0 -> x14, waiting for transfers between devices: none -> 25.8 us  [swap(): return lax.ppermute(array, 'vel', [(i, i ^ bits) for i in range(axis_size)])]
    pallas_call x0 -> x3, Pallas kernels: none -> 20.2 us  [the longest x1 15.9 us: local(): pl.pallas_call(functools.partial(stack_kernel, block, rows, per_device, e...]
    ppermute x0 -> x14, starting transfers between devices: none -> 20.1 us  [swap(): return lax.ppermute(array, 'vel', [(i, i ^ bits) for i in range(axis_size)])]
    select_n x8 -> x0, other arithmetic: 10.9 us -> none  [shift_bands(): times[:, None] * rate_rows[None, :, 0] // rate_divisor]
    slice x8 -> x2, local copies, waits for them, and re-layouts: 10.7 us -> 0.06 us  [the longest x1 0.04 us: local(): other = jnp.concatenate([other[chips:], other[:chips]])]
  transfers between devices with their start and end apart: 2 -> 14, of which waited for: 2 -> 10; matrix products, arithmetic and copies ran while one was open for 0% -> 0% of each run, Pallas kernels for 0% -> 0%
where the time goes in v1:
time: 71.7 us; the launch traced here: 71.4 us
  waiting for transfers between devices  25.8 us (36%)
  Pallas kernels  20.2 us (28%)
  starting transfers between devices  20.1 us (28%)
  local copies, waits for them, and re-layouts  3.62 us (5%)
  other arithmetic  0.89 us (1%)
  between operations  0.76 us (1%)
    ppermute x14, waiting for transfers between devices, swap(): return lax.ppermute(array, 'vel', [(i, i ^ bits) for i in range(axis_size)])  25.8 us
    ppermute x14, starting transfers between devices, swap(): return lax.ppermute(array, 'vel', [(i, i ^ bits) for i in range(axis_size)])  20.1 us
    pallas_call x1, Pallas kernels, local(): pl.pallas_call(functools.partial(stack_kernel, block, rows, per_device, e...  15.9 us
    unnamed x16, local copies, waits for them, and re-layouts  3.49 us
    pallas_call x1, Pallas kernels, local(): pl.pallas_call(functools.partial(window_kernel, block, chips), out_shape=...  2.45 us
    pallas_call x1, Pallas kernels, local(): pl.pallas_call(functools.partial(assemble_kernel, block), out_shape=[jax....  1.85 us
  transfers between devices with their start and end apart: 14, of which 10 were waited for; matrix products, arithmetic and copies ran while one was open for 0% of the time, Pallas kernels for 0%

profile of v1, /device:TPU:0, one launch (start us, length us, event | category | flops | bytes accessed | tf_op | source)
XLA Modules:
  0.0 71.4 jit_solution(9571691986255258300)
XLA Ops:
  0.7 2.4 %windows.1 = (bf16[192,768]{1,0:T(8,128)(2,1)}, bf16[192,768]{1,0:T(8,128)(2,1)}, bf16[192,768]{1,0:T(8,128)(2,1)}, bf16[192,768]{1,0:T(8,128)(2,1)}) custom-call(s32[1]{0:T(128)} %bitcast.place_ref, bf16[768,512]{1,0:T(8,128)(2,1)} %bitcast.15), custom_call_target="tpu_custom_call" | custom-call | tf_op jit(solution)/shard_map/windows/pallas_call | solution.py:123
  3.1 3.0 %collective-permute-start.5 = (bf16[192,768]{1,0:T(8,128)(2,1)}, bf16[192,768]{1,0:T(8,128)(2,1)S(1)}, u32[]{:S(2)}, u32[]{:S(2)}) collective-permute-start(bf16[192,768]{1,0:T(8,128)(2,1)} %get-tuple-element.7), channel_id=1, source_target_pairs={{0,2},{1,3},{2,0},{3,1},{4,6},{5,7},{6,4},{7,5},{8,10},{9,11},{10,... | collective-permute-start | bytes 884744 | tf_op jit(solution)/shard_map/ppermute | solution.py:117
  6.1 0.0 copy-start.7
  6.1 1.6 %collective-permute-start.6 = (bf16[192,768]{1,0:T(8,128)(2,1)}, bf16[192,768]{1,0:T(8,128)(2,1)S(1)}, u32[]{:S(2)}, u32[]{:S(2)}) collective-permute-start(bf16[192,768]{1,0:T(8,128)(2,1)} %get-tuple-element.8), channel_id=1, source_target_pairs={{0,4},{1,5},{2,6},{3,7},{4,0},{5,1},{6,2},{7,3},{8,12},{9,13},{10,... | collective-permute-start | bytes 884744 | tf_op jit(solution)/shard_map/ppermute | solution.py:117
  7.7 0.0 collective-permute-start.7
  7.7 0.0 copy-done.7
  7.7 0.0 collective-permute-start
  7.7 1.1 %collective-permute-done = s32[1,2]{1,0:T(1,128)S(1)} collective-permute-done((s32[1,2]{1,0:T(1,128)S(1)}, s32[1,2]{1,0:T(1,128)S(1)}, u32[]{:S(2)}, u32[]{:S(2)}) %collective-permute-start) | collective-permute-done | bytes 40 | tf_op jit(solution)/shard_map/ppermute | solution.py:117
  8.8 2.0 %collective-permute-start.1 = (s32[2,2]{1,0:T(2,128)S(1)}, s32[2,2]{1,0:T(2,128)S(1)}, u32[]{:S(2)}, u32[]{:S(2)}) collective-permute-start(s32[2,2]{1,0:T(2,128)S(1)} %pad_add_fusion), channel_id=1, source_target_pairs={{0,2},{1,3},{2,0},{3,1},{4,6},{5,7},{6,4},{7,5},{8,10},{9,11},{10,... | collective-permute-start | bytes 56 | tf_op jit(solution)/shard_map/ppermute | solution.py:117
  10.8 1.6 %collective-permute-start.2 = (s32[2,2]{1,0:T(2,128)S(1)}, s32[2,2]{1,0:T(2,128)S(1)}, u32[]{:S(2)}, u32[]{:S(2)}) collective-permute-start(s32[2,2]{1,0:T(2,128)S(1)} %pad_add_fusion), channel_id=1, source_target_pairs={{0,4},{1,5},{2,6},{3,7},{4,0},{5,1},{6,2},{7,3},{8,12},{9,13},{10,... | collective-permute-start | bytes 56 | tf_op jit(solution)/shard_map/ppermute | solution.py:117
  12.3 1.0 %collective-permute-done.1 = s32[2,2]{1,0:T(2,128)S(1)} collective-permute-done((s32[2,2]{1,0:T(2,128)S(1)}, s32[2,2]{1,0:T(2,128)S(1)}, u32[]{:S(2)}, u32[]{:S(2)}) %collective-permute-start.1) | collective-permute-done | bytes 48 | tf_op jit(solution)/shard_map/ppermute | solution.py:117
  13.4 3.1 %collective-permute-start.3 = (s32[2,2]{1,0:T(2,128)S(1)}, s32[2,2]{1,0:T(2,128)S(1)}, u32[]{:S(2)}, u32[]{:S(2)}) collective-permute-start(s32[2,2]{1,0:T(2,128)S(1)} %pad_add_fusion), channel_id=1, source_target_pairs={{0,6},{1,7},{2,4},{3,5},{4,2},{5,3},{6,0},{7,1},{8,14},{9,15},{10,... | collective-permute-start | bytes 56 | tf_op jit(solution)/shard_map/ppermute | solution.py:117
  16.4 4.7 %collective-permute-done.2 = s32[2,2]{1,0:T(2,128)S(1)} collective-permute-done((s32[2,2]{1,0:T(2,128)S(1)}, s32[2,2]{1,0:T(2,128)S(1)}, u32[]{:S(2)}, u32[]{:S(2)}) %collective-permute-start.2) | collective-permute-done | bytes 48 | tf_op jit(solution)/shard_map/ppermute | solution.py:117
  21.1 0.0 collective-permute-done.3
  21.1 2.6 %collective-permute-start.4 = (s32[8,2]{1,0:T(8,128)S(1)}, s32[8,2]{1,0:T(8,128)S(1)}, u32[]{:S(2)}, u32[]{:S(2)}) collective-permute-start(s32[8,2]{1,0:T(8,128)S(1)} %concatenate.15), channel_id=1, source_target_pairs={{0,8},{1,9},{2,10},{3,11},{4,12},{5,13},{6,14},{7,15},{8,0},{9,1},... | collective-permute-start | bytes 200 | tf_op jit(solution)/shard_map/ppermute | solution.py:117
  23.8 1.9 %collective-permute-done.4 = s32[8,2]{1,0:T(8,128)S(1)} collective-permute-done((s32[8,2]{1,0:T(8,128)S(1)}, s32[8,2]{1,0:T(8,128)S(1)}, u32[]{:S(2)}, u32[]{:S(2)}) %collective-permute-start.4) | collective-permute-done | bytes 96 | tf_op jit(solution)/shard_map/ppermute | solution.py:117
  25.7 0.0 collective-permute-done.5.refs_1_
  25.7 0.0 collective-permute-done.6.refs_2_
  25.7 0.0 collective-permute-done.7.refs_3_
  25.7 0.0 copy-start.2
  25.8 0.0 copy-start.3
  25.8 0.6 copy-done.2
  26.4 0.0 copy-done.3
  26.4 0.0 copy-start
  26.4 1.2 %copy-done = bf16[4,256,512]{2,1,0:T(8,128)(2,1)S(1)} copy-done((bf16[4,256,512]{2,1,0:T(8,128)(2,1)S(1)}, bf16[4,256,512]{2,1,0:T(8,128)(2,1)}, u32[]{:S(2)}) %copy-start) | copy-done | bytes 1048600
  27.6 0.0 copy-start.1
  27.6 1.0 %copy-done.1 = bf16[192,768]{1,0:T(8,128)(2,1)S(1)} copy-done((bf16[192,768]{1,0:T(8,128)(2,1)S(1)}, bf16[192,768]{1,0:T(8,128)(2,1)}, u32[]{:S(2)}) %copy-start.1) | copy-done | bytes 294936
  28.6 15.9 %stack.24 = f32[2,8,96,128]{3,2,1,0:T(8,128)S(1)} custom-call(s32[1]{0:T(128)} %bitcast.1.device_ref, s32[16,2]{1,0:T(8,128)S(1)} %concatenate.16.velocity_ref, s32[64]{0:T(128)S(1)} %copy-done.2, s32[64]{0:T(128)S(1)} %copy-done.3, bf16[4,256,512]{2,1,0:T(8,128)(2,1)S(1)} %copy-done, bf16[192,768]{1,0:T(8,128)(2,1)S(1)} %copy-done.1, ...), custom_call_target="tpu_custom_call" | custom-call | tf_op jit(solution)/shard_map/stack/pallas_call | solution.py:139
  44.6 0.1 collective-permute-start.8
  44.7 1.7 %collective-permute-done.8 = f32[8,96,128]{2,1,0:T(8,128)S(1)} collective-permute-done((f32[8,96,128]{2,1,0:T(8,128)S(1)}, f32[8,96,128]{2,1,0:T(8,128)S(1)}, u32[]{:S(2)}, u32[]{:S(2)}) %collective-permute-start.8) | collective-permute-done | bytes 393248 | tf_op jit(solution)/shard_map/ppermute | solution.py:117
  46.4 0.1 fusion.2
  46.4 2.6 %collective-permute-start.9 = (f16[8,96,128]{2,1,0:T(8,128)(2,1)S(1)}, f16[8,96,128]{2,1,0:T(8,128)(2,1)S(1)}, u32[]{:S(2)}, u32[]{:S(2)}) collective-permute-start(f16[8,96,128]{2,1,0:T(8,128)(2,1)S(1)} %fusion.2), channel_id=1, source_target_pairs={{0,8},{1,9},{2,10},{3,11},{4,12},{5,13},{6,14},{7,15},{8,0},{9,1},... | collective-permute-start | bytes 589832 | tf_op jit(solution)/shard_map/ppermute | solution.py:117
  49.1 9.5 %collective-permute-done.9 = f16[8,96,128]{2,1,0:T(8,128)(2,1)S(1)} collective-permute-done((f16[8,96,128]{2,1,0:T(8,128)(2,1)S(1)}, f16[8,96,128]{2,1,0:T(8,128)(2,1)S(1)}, u32[]{:S(2)}, u32[]{:S(2)}) %collective-permute-start.9) | collective-permute-done | bytes 196640 | tf_op jit(solution)/shard_map/ppermute | solution.py:117
  58.6 0.1 fusion.3
  58.8 0.1 collective-permute-start.10
  58.9 1.2 %collective-permute-done.10 = f32[96,128]{1,0:T(8,128)S(1)} collective-permute-done((f32[96,128]{1,0:T(8,128)S(1)}, f32[96,128]{1,0:T(8,128)S(1)}, u32[]{:S(2)}, u32[]{:S(2)}) %collective-permute-start.10) | collective-permute-done | bytes 49184 | tf_op jit(solution)/shard_map/ppermute | solution.py:117
  60.1 0.7 pad_maximum_fusion
  60.7 1.5 %collective-permute-start.11 = (f32[2,96,128]{2,1,0:T(8,128)S(1)}, f32[2,96,128]{2,1,0:T(8,128)S(1)}, u32[]{:S(2)}, u32[]{:S(2)}) collective-permute-start(f32[2,96,128]{2,1,0:T(8,128)S(1)} %get-tuple-element.19), channel_id=1, source_target_pairs={{0,2},{1,3},{2,0},{3,1},{4,6},{5,7},{6,4},{7,5},{8,10},{9,11},{10,... | collective-permute-start | bytes 294920 | tf_op jit(solution)/shard_map/ppermute | solution.py:117
  62.2 0.7 collective-permute-start.12
  62.9 1.3 %collective-permute-start.13 = (f32[2,96,128]{2,1,0:T(8,128)S(1)}, f32[2,96,128]{2,1,0:T(8,128)S(1)}, u32[]{:S(2)}, u32[]{:S(2)}) collective-permute-start(f32[2,96,128]{2,1,0:T(8,128)S(1)} %get-tuple-element.18), channel_id=1, source_target_pairs={{0,6},{1,7},{2,4},{3,5},{4,2},{5,3},{6,0},{7,1},{8,14},{9,15},{10,... | collective-permute-start | bytes 294920 | tf_op jit(solution)/shard_map/ppermute | solution.py:117
  64.2 1.4 %collective-permute-done.11.refs_1_ = f32[2,96,128]{2,1,0:T(8,128)S(1)} collective-permute-done((f32[2,96,128]{2,1,0:T(8,128)S(1)}, f32[2,96,128]{2,1,0:T(8,128)S(1)}, u32[]{:S(2)}, u32[]{:S(2)}) %collective-permute-start.11) | collective-permute-done | bytes 98336 | tf_op jit(solution)/shard_map/ppermute | solution.py:117
  65.6 0.0 copy-start.4
  65.6 2.3 %collective-permute-done.12.refs_2_ = f32[2,96,128]{2,1,0:T(8,128)S(1)} collective-permute-done((f32[2,96,128]{2,1,0:T(8,128)S(1)}, f32[2,96,128]{2,1,0:T(8,128)S(1)}, u32[]{:S(2)}, u32[]{:S(2)}) %collective-permute-start.12) | collective-permute-done | bytes 98336 | tf_op jit(solution)/shard_map/ppermute | solution.py:117
  67.9 0.0 copy-start.5
  67.9 1.0 %collective-permute-done.13.refs_3_ = f32[2,96,128]{2,1,0:T(8,128)S(1)} collective-permute-done((f32[2,96,128]{2,1,0:T(8,128)S(1)}, f32[2,96,128]{2,1,0:T(8,128)S(1)}, u32[]{:S(2)}, u32[]{:S(2)}) %collective-permute-start.13) | collective-permute-done | bytes 98336 | tf_op jit(solution)/shard_map/ppermute | solution.py:117
  68.9 0.0 copy-start.6
  68.9 0.0 copy-done.4
  68.9 0.0 copy-done.5
  68.9 0.6 copy-done.6
  69.6 1.9 %assemble.1 = (f32[1,96,512]{2,1,0:T(8,128)}, f32[96,512]{1,0:T(8,128)}) custom-call(s32[1]{0:T(128)} %bitcast.place_ref, f32[2,96,128]{2,1,0:T(8,128)} %get-tuple-element.21.refs_0_, f32[2,96,128]{2,1,0:T(8,128)} %copy-done.4, f32[2,96,128]{2,1,0:T(8,128)} %copy-done.5, f32[2,96,128]{2,1,0:T(8,128)} %copy-done.6), custom_call_target="tpu_custom_call" | custom-call | tf_op jit(solution)/shard_map/assemble/pallas_call | solution.py:165
  (7 shorter events, 0.1 us)
Async XLA Ops:
  3.1 22.6 %collective-permute-start.5 = (bf16[192,768]{1,0:T(8,128)(2,1)}, bf16[192,768]{1,0:T(8,128)(2,1)S(1)}, u32[]{:S(2)}, u32[]{:S(2)}) collective-permute-start(bf16[192,768]{1,0:T(8,128)(2,1)} %get-tuple-element.7), channel_id=1, source_target_pairs={{0,2},{1,3},{2,0},{3,1},{4,6},{5,7},{6,4},{7,5},{8,10},{9,11},{10,... | collective-permute-start | bytes 884744 | tf_op jit(solution)/shard_map/ppermute | solution.py:117
  6.1 1.6 %copy-start.7 = (s32[1,2]{1,0:T(1,128)S(1)}, s32[1,2]{1,0:T(1,128)}, u32[]{:S(2)}) copy-start(s32[1,2]{1,0:T(1,128)} %param.6) | copy-start | bytes 28
  6.1 19.6 %collective-permute-start.6 = (bf16[192,768]{1,0:T(8,128)(2,1)}, bf16[192,768]{1,0:T(8,128)(2,1)S(1)}, u32[]{:S(2)}, u32[]{:S(2)}) collective-permute-start(bf16[192,768]{1,0:T(8,128)(2,1)} %get-tuple-element.8), channel_id=1, source_target_pairs={{0,4},{1,5},{2,6},{3,7},{4,0},{5,1},{6,2},{7,3},{8,12},{9,13},{10,... | collective-permute-start | bytes 884744 | tf_op jit(solution)/shard_map/ppermute | solution.py:117
  7.7 18.1 %collective-permute-start.7 = (bf16[192,768]{1,0:T(8,128)(2,1)}, bf16[192,768]{1,0:T(8,128)(2,1)S(1)}, u32[]{:S(2)}, u32[]{:S(2)}) collective-permute-start(bf16[192,768]{1,0:T(8,128)(2,1)} %get-tuple-element.9), channel_id=1, source_target_pairs={{0,6},{1,7},{2,4},{3,5},{4,2},{5,3},{6,0},{7,1},{8,14},{9,15},{10,... | collective-permute-start | bytes 884744 | tf_op jit(solution)/shard_map/ppermute | solution.py:117
  7.7 1.1 %collective-permute-start = (s32[1,2]{1,0:T(1,128)S(1)}, s32[1,2]{1,0:T(1,128)S(1)}, u32[]{:S(2)}, u32[]{:S(2)}) collective-permute-start(s32[1,2]{1,0:T(1,128)S(1)} %copy-done.7), channel_id=1, source_target_pairs={{0,1},{1,0},{2,3},{3,2},{4,5},{5,4},{6,7},{7,6},{8,9},{9,8},{10,11... | collective-permute-start | bytes 32 | tf_op jit(solution)/shard_map/ppermute | solution.py:117
  8.8 4.6 %collective-permute-start.1 = (s32[2,2]{1,0:T(2,128)S(1)}, s32[2,2]{1,0:T(2,128)S(1)}, u32[]{:S(2)}, u32[]{:S(2)}) collective-permute-start(s32[2,2]{1,0:T(2,128)S(1)} %pad_add_fusion), channel_id=1, source_target_pairs={{0,2},{1,3},{2,0},{3,1},{4,6},{5,7},{6,4},{7,5},{8,10},{9,11},{10,... | collective-permute-start | bytes 56 | tf_op jit(solution)/shard_map/ppermute | solution.py:117
  10.8 10.3 %collective-permute-start.2 = (s32[2,2]{1,0:T(2,128)S(1)}, s32[2,2]{1,0:T(2,128)S(1)}, u32[]{:S(2)}, u32[]{:S(2)}) collective-permute-start(s32[2,2]{1,0:T(2,128)S(1)} %pad_add_fusion), channel_id=1, source_target_pairs={{0,4},{1,5},{2,6},{3,7},{4,0},{5,1},{6,2},{7,3},{8,12},{9,13},{10,... | collective-permute-start | bytes 56 | tf_op jit(solution)/shard_map/ppermute | solution.py:117
  13.4 7.8 %collective-permute-start.3 = (s32[2,2]{1,0:T(2,128)S(1)}, s32[2,2]{1,0:T(2,128)S(1)}, u32[]{:S(2)}, u32[]{:S(2)}) collective-permute-start(s32[2,2]{1,0:T(2,128)S(1)} %pad_add_fusion), channel_id=1, source_target_pairs={{0,6},{1,7},{2,4},{3,5},{4,2},{5,3},{6,0},{7,1},{8,14},{9,15},{10,... | collective-permute-start | bytes 56 | tf_op jit(solution)/shard_map/ppermute | solution.py:117
  21.1 4.6 %collective-permute-start.4 = (s32[8,2]{1,0:T(8,128)S(1)}, s32[8,2]{1,0:T(8,128)S(1)}, u32[]{:S(2)}, u32[]{:S(2)}) collective-permute-start(s32[8,2]{1,0:T(8,128)S(1)} %concatenate.15), channel_id=1, source_target_pairs={{0,8},{1,9},{2,10},{3,11},{4,12},{5,13},{6,14},{7,15},{8,0},{9,1},... | collective-permute-start | bytes 200 | tf_op jit(solution)/shard_map/ppermute | solution.py:117
  25.7 0.7 copy-start.2
  25.8 0.7 copy-start.3
  26.4 1.2 %copy-start = (bf16[4,256,512]{2,1,0:T(8,128)(2,1)S(1)}, bf16[4,256,512]{2,1,0:T(8,128)(2,1)}, u32[]{:S(2)}) copy-start(bf16[4,256,512]{2,1,0:T(8,128)(2,1)} %constant.40.clone.filter_ref) | copy-start | bytes 3145732
  27.6 1.0 %copy-start.1 = (bf16[192,768]{1,0:T(8,128)(2,1)S(1)}, bf16[192,768]{1,0:T(8,128)(2,1)}, u32[]{:S(2)}) copy-start(bf16[192,768]{1,0:T(8,128)(2,1)} %get-tuple-element.6.refs_0_) | copy-start | bytes 884740
  44.6 1.8 %collective-permute-start.8 = (f32[8,96,128]{2,1,0:T(8,128)S(1)}, f32[8,96,128]{2,1,0:T(8,128)S(1)}, u32[]{:S(2)}, u32[]{:S(2)}) collective-permute-start(f32[8,96,128]{2,1,0:T(8,128)S(1)} %slice_bitcast_fusion), channel_id=1, source_target_pairs={{0,1},{1,0},{2,3},{3,2},{4,5},{5,4},{6,7},{7,6},{8,9},{9,8},{10,11... | collective-permute-start | bytes 1179656 | tf_op jit(solution)/shard_map/ppermute | solution.py:117
  46.4 12.1 %collective-permute-start.9 = (f16[8,96,128]{2,1,0:T(8,128)(2,1)S(1)}, f16[8,96,128]{2,1,0:T(8,128)(2,1)S(1)}, u32[]{:S(2)}, u32[]{:S(2)}) collective-permute-start(f16[8,96,128]{2,1,0:T(8,128)(2,1)S(1)} %fusion.2), channel_id=1, source_target_pairs={{0,8},{1,9},{2,10},{3,11},{4,12},{5,13},{6,14},{7,15},{8,0},{9,1},... | collective-permute-start | bytes 589832 | tf_op jit(solution)/shard_map/ppermute | solution.py:117
  58.8 1.3 %collective-permute-start.10 = (f32[96,128]{1,0:T(8,128)S(1)}, f32[96,128]{1,0:T(8,128)S(1)}, u32[]{:S(2)}, u32[]{:S(2)}) collective-permute-start(f32[96,128]{1,0:T(8,128)S(1)} %get-tuple-element.10), channel_id=1, source_target_pairs={{0,1},{1,0},{2,3},{3,2},{4,5},{5,4},{6,7},{7,6},{8,9},{9,8},{10,11... | collective-permute-start | bytes 147464 | tf_op jit(solution)/shard_map/ppermute | solution.py:117
  60.7 4.9 %collective-permute-start.11 = (f32[2,96,128]{2,1,0:T(8,128)S(1)}, f32[2,96,128]{2,1,0:T(8,128)S(1)}, u32[]{:S(2)}, u32[]{:S(2)}) collective-permute-start(f32[2,96,128]{2,1,0:T(8,128)S(1)} %get-tuple-element.19), channel_id=1, source_target_pairs={{0,2},{1,3},{2,0},{3,1},{4,6},{5,7},{6,4},{7,5},{8,10},{9,11},{10,... | collective-permute-start | bytes 294920 | tf_op jit(solution)/shard_map/ppermute | solution.py:117
  62.2 5.6 %collective-permute-start.12 = (f32[2,96,128]{2,1,0:T(8,128)S(1)}, f32[2,96,128]{2,1,0:T(8,128)S(1)}, u32[]{:S(2)}, u32[]{:S(2)}) collective-permute-start(f32[2,96,128]{2,1,0:T(8,128)S(1)} %get-tuple-element.20), channel_id=1, source_target_pairs={{0,4},{1,5},{2,6},{3,7},{4,0},{5,1},{6,2},{7,3},{8,12},{9,13},{10,... | collective-permute-start | bytes 294920 | tf_op jit(solution)/shard_map/ppermute | solution.py:117
  62.9 6.0 %collective-permute-start.13 = (f32[2,96,128]{2,1,0:T(8,128)S(1)}, f32[2,96,128]{2,1,0:T(8,128)S(1)}, u32[]{:S(2)}, u32[]{:S(2)}) collective-permute-start(f32[2,96,128]{2,1,0:T(8,128)S(1)} %get-tuple-element.18), channel_id=1, source_target_pairs={{0,6},{1,7},{2,4},{3,5},{4,2},{5,3},{6,0},{7,1},{8,14},{9,15},{10,... | collective-permute-start | bytes 294920 | tf_op jit(solution)/shard_map/ppermute | solution.py:117
  65.6 3.3 %copy-start.4 = (f32[2,96,128]{2,1,0:T(8,128)}, f32[2,96,128]{2,1,0:T(8,128)S(1)}, u32[]{:S(2)}) copy-start(f32[2,96,128]{2,1,0:T(8,128)S(1)} %collective-permute-done.11.refs_1_) | copy-start | bytes 294916
  67.9 1.0 %copy-start.5 = (f32[2,96,128]{2,1,0:T(8,128)}, f32[2,96,128]{2,1,0:T(8,128)S(1)}, u32[]{:S(2)}) copy-start(f32[2,96,128]{2,1,0:T(8,128)S(1)} %collective-permute-done.12.refs_2_) | copy-start | bytes 294916
  68.9 0.6 copy-start.6

commit v2 on v0

v2 whole, which is shorter than its diff:
```python
import functools

import jax
import jax.numpy as jnp
import ml_dtypes
import numpy as np
from jax import lax
from jax.experimental import pallas as pl
from jax.experimental.pallas import tpu as pltpu
from jax.sharding import PartitionSpec as P

SPLINE = np.array(
    [
        [64.0, 256.0, 64.0, 0.0],
        [27.0, 235.0, 121.0, 1.0],
        [8.0, 184.0, 184.0, 8.0],
        [1.0, 121.0, 235.0, 27.0],
    ],
    np.float32,
)
spline_norm = 147456.0
rate_divisor = 32
HALO = 24
LANES = 128
PACK = 16
LINK_SCALE = 64.0


def row_filter(rows):
    band = np.zeros((rows, 4 * LANES), np.float32)
    for row in range(rows):
        for tap in range(4):
            for fraction in range(4):
                band[row, fraction * LANES + (row - tap + 1) % LANES] = SPLINE[fraction, tap]
    return band.astype(ml_dtypes.bfloat16)


def window_kernel(block, chips, place_ref, image_ref, *refs):
    *window_refs, padded = refs
    lanes, columns = image_ref.shape
    image = jnp.concatenate([image_ref[...], jnp.zeros((lanes, LANES), image_ref.dtype)], axis=1)
    image = pltpu.roll(image, HALO, 1)
    for first in range(0, columns + LANES, LANES):
        padded[first : first + LANES] = image[:, first : first + LANES].T
    for relative, window_ref in enumerate(window_refs):
        start = pl.multiple_of((place_ref[0] ^ relative) * block, block)
        window_ref[...] = padded[pl.ds(start, block + 2 * HALO)]


def stack_kernel(block, rows, sources, images, first, scale, carried, time_ref, rate_ref, filter_ref, *refs):
    window_refs, before, refs = refs[: len(sources)], refs[len(sources) :][:carried], refs[len(sources) + carried :]
    keep_ref, send_ref, bands, filtered, *bins = refs
    lanes = window_refs[0].shape[1]
    together = len(bins)
    turns = bins[0].shape[0] // 4
    reach = bins[0].shape[1] - PACK
    wide = window_refs[0].shape[0]
    offsets = sorted({rows * number % LANES for number in range(images)})
    bands[...] = jnp.zeros(bands.shape, bands.dtype)
    for number, offset in enumerate(offsets):
        bands[number, offset : offset + rows] = filter_ref[...]
    for part in bins:
        part[...] = jnp.zeros(part.shape, part.dtype)
    if filtered.shape[2] > wide:
        filtered[:, :, wide:] = jnp.zeros((*filtered.shape[:2], filtered.shape[2] - wide, LANES), filtered.dtype)
    for index, (relative, window_ref) in enumerate(zip(sources, window_refs)):
        for number in range(images):
            time = time_ref[relative * images + number]
            held = index * images + number
            low = rows * number // LANES * LANES
            high = min(lanes, (rows * (number + 1) + LANES - 1) // LANES * LANES)
            band = bands[offsets.index(rows * number - low), : high - low]
            product = jnp.dot(window_ref[:, low:high], band, preferred_element_type=jnp.float32)
            product = product.astype(jnp.bfloat16)
            for fraction in range(4):
                filtered[held, fraction, :wide] = product[:, fraction * LANES : (fraction + 1) * LANES]

            def add(turn, _, time=time, held=held):
                for lane in range(together):
                    v = first + turn * together + lane
                    row_offset = (rate_ref[v, 0] * time) >> 5
                    column_offset = (rate_ref[v, 1] * time) >> 5
                    start = HALO - 1 + (column_offset >> 2)
                    even = pl.multiple_of((start >> 4) << 4, PACK)
                    shifted = filtered[held, row_offset & 3, pl.ds(even, reach), :]
                    shifted = pltpu.roll(shifted, (LANES - (row_offset >> 2)) & (LANES - 1), 1)
                    place = 4 * turn + (column_offset & 3)
                    bins[lane][place, pl.ds(PACK - (start - even), reach), :] += shifted.astype(jnp.float32)
                return _

            if turns == 1:
                add(0, 0)
            else:
                lax.fori_loop(0, turns, add, 0)

    def finish(turn, _):
        for lane in range(together):
            v = turn * together + lane
            total = jnp.zeros((block, LANES), jnp.float32)
            for fraction in range(4):
                for tap in range(4):
                    if SPLINE[fraction, tap]:
                        taken = bins[lane][4 * turn + fraction, PACK + tap : PACK + tap + block, :]
                        total = total + float(SPLINE[fraction, tap]) * taken
            total = (total * scale).T[:rows]
            if before:
                total = total + before[lane & 1][v >> 1]
            (send_ref if lane & 1 else keep_ref)[v >> 1] = total
        return _

    if turns == 1:
        finish(0, 0)
    else:
        lax.fori_loop(0, turns, finish, 0)


def arrange(pieces, place):
    step = 1
    while step < len(pieces):
        flip = (place & step) != 0
        pieces = [jnp.where(flip, pieces[x ^ step], pieces[x]) for x in range(len(pieces))]
        step *= 2
    return jnp.concatenate(pieces, axis=-1)


def local(axis_size, epoch_maps, velocity, slot_epoch, epoch_time):
    per_device, rows, columns = epoch_maps.shape
    epochs = slot_epoch.shape[0]
    half = axis_size // 2
    chips = half // 2
    block = columns // chips
    device = lax.axis_index("vel").astype(jnp.int32)
    place = device % half // 2

    def swap(array, bits):
        return lax.ppermute(array, "vel", [(i, i ^ bits) for i in range(axis_size)])

    smem = pl.BlockSpec(memory_space=pltpu.SMEM)
    vmem = pl.BlockSpec(memory_space=pltpu.VMEM)
    lanes = per_device * rows
    wide = block + 2 * HALO
    shape = jax.ShapeDtypeStruct

    windows = pl.pallas_call(
        functools.partial(window_kernel, block, chips),
        out_shape=[shape((wide, lanes), epoch_maps.dtype)] * chips,
        in_specs=[smem, vmem],
        out_specs=[vmem] * chips,
        scratch_shapes=[pltpu.VMEM((columns + LANES, lanes), epoch_maps.dtype)],
        name="windows",
    )(place.reshape(1), epoch_maps.reshape(lanes, columns))

    rates = jnp.concatenate([velocity] + [swap(velocity, 2 * x) for x in range(1, chips)])
    windows, rates = lax.optimization_barrier((windows, rates))
    rates = jnp.concatenate([rates, swap(rates, half)])
    rates = jnp.stack([rates, swap(rates, 1)], axis=1).reshape(axis_size, 2)
    windows = [windows[0]] + [swap(windows[x], 2 * x) for x in range(1, chips)]

    source = device ^ (2 * jnp.arange(chips, dtype=jnp.int32))
    slot = (source[:, None] * per_device + jnp.arange(per_device, dtype=jnp.int32)) % epochs
    every = jnp.arange(epochs, dtype=jnp.int32)
    epoch = jnp.sum(jnp.where(slot[..., None] == every, slot_epoch, 0), axis=-1)
    times = jnp.sum(jnp.where(epoch[..., None] == every, epoch_time, 0), axis=-1).reshape(-1)

    reach = (block + 2 + PACK + PACK - 1) // PACK * PACK
    band = jnp.asarray(row_filter(rows))

    def stack(sources, first, count, carried=()):
        together = min(count, 16)
        tall = max(wide, 2 * PACK + reach)
        return pl.pallas_call(
            functools.partial(
                stack_kernel, block, rows, sources, per_device, first, LINK_SCALE / spline_norm, len(carried)
            ),
            out_shape=[shape((count // 2, rows, block), jnp.float32)] * 2,
            in_specs=[smem] * 2 + [vmem] * (1 + len(sources) + len(carried)),
            out_specs=[vmem] * 2,
            scratch_shapes=[
                pltpu.VMEM((4, 2 * LANES, 4 * LANES), jnp.bfloat16),
                pltpu.VMEM((len(sources) * per_device, 4, tall, LANES), jnp.bfloat16),
            ]
            + [pltpu.VMEM((4 * count // together, reach + PACK, LANES), jnp.float32)] * together,
            compiler_params=pltpu.CompilerParams(vmem_limit_bytes=40 * 1024 * 1024),
            name="stack",
        )(times, rates, band, *[windows[x] for x in sources], *carried)

    late = [chips - 1]
    early = [x for x in range(1, chips) if x not in late]
    keep, send = stack([0], 0, axis_size)
    if early:
        keep, send = stack(early, 0, axis_size, (keep, send))
    keep_far, send_far = stack(late, half, half, (keep[chips:], send[chips:]))
    far = (keep_far + swap(send_far, 1)).astype(jnp.float16)
    near = (keep[:chips], send[:chips])
    far, near = lax.optimization_barrier((far, near))
    other = swap(far, half).astype(jnp.float32) * (1.0 / LINK_SCALE)
    keep_near, send_near = stack(late, 0, half, near)
    near = (keep_near + swap(send_near, 1)) * (1.0 / LINK_SCALE)
    first = device < half
    near = jnp.where(first, near, other) / jnp.sqrt(jnp.where(first, other, near) + 1.0)
    best = jnp.max(near, axis=0)
    best = jnp.maximum(jnp.maximum(best, swap(best, 1)), jnp.maximum(swap(best, half), swap(best, half + 1)))

    pieces = [(jnp.concatenate([near[x], best]) * LINK_SCALE).astype(jnp.float16) for x in range(chips)]
    pieces = [pieces[0]] + [swap(pieces[x], 2 * x) for x in range(1, chips)]
    whole = arrange(pieces, place).astype(jnp.float32) * (1.0 / LINK_SCALE)
    return whole[None, :rows], whole[rows:]


def solution(mesh):
    return jax.shard_map(
        functools.partial(local, mesh.shape["vel"]),
        mesh=mesh,
        in_specs=(P("vel", "groups", None), P("vel", None), P(), P()),
        out_specs=(P("vel", "groups", None), P("groups", None)),
        check_vma=False,
    )
```

time: 284 us -> 60.5 us (0.21)
  waiting for transfers between devices: 194 us -> 18.2 us
  matrix products: 48.5 us -> 0 us
  Pallas kernels: 0 us -> 18.5 us
  starting transfers between devices: 0.08 us -> 18 us
  between operations: 14.1 us -> 0.77 us
  other arithmetic: 13.9 us -> 1.05 us
  local copies, waits for them, and re-layouts: 12.3 us -> 3.73 us
    all_gather x1 -> x0, waiting for transfers between devices: 105 us -> none  [local(): gathered = lax.all_gather(epoch_maps, 'vel', axis=0, tiled=True)]
    pmax x1 -> x0, waiting for transfers between devices: 88.1 us -> none  [local(): best_value = lax.pmax(jnp.max(likelihood, axis=0), 'vel')]
    dot_general x8 -> x0, matrix products: 48.5 us -> none  [one_block(): jnp.einsum('pvmoj,pvcj->vmoc', rows_done, column_band, preferred_element_...]
    pallas_call x0 -> x5, Pallas kernels: none -> 18.5 us  [the longest x4 15.7 us: stack(): pl.pallas_call(functools.partial(stack_kernel, block, rows, sources, per_...]
    ppermute x0 -> x17, waiting for transfers between devices: none -> 18.2 us  [swap(): return lax.ppermute(array, 'vel', [(i, i ^ bits) for i in range(axis_size)])]
    ppermute x0 -> x17, starting transfers between devices: none -> 18 us  [swap(): return lax.ppermute(array, 'vel', [(i, i ^ bits) for i in range(axis_size)])]
    select_n x8 -> x3, other arithmetic: 10.9 us -> 0.18 us  [the longest x2 0.1 us: arrange(): jnp.where(flip, pieces[x ^ step], pieces[x])]
    slice x8 -> x2, local copies, waits for them, and re-layouts: 10.7 us -> 0.82 us  [the longest x1 0.77 us: local(): return (whole[None, :rows], whole[rows:])]
  transfers between devices with their start and end apart: 2 -> 17, of which waited for: 2 -> 8; matrix products, arithmetic and copies ran while one was open for 0% -> 2% of each run, Pallas kernels for 0% -> 22%
where the time goes in v2:
time: 60.5 us; the launch traced here: 60.3 us
  Pallas kernels  18.5 us (31%)
  waiting for transfers between devices  18.2 us (30%)
  starting transfers between devices  18 us (30%)
  local copies, waits for them, and re-layouts  3.73 us (6%)
  other arithmetic  1.05 us (2%)
  between operations  0.77 us (1%)
    ppermute x17, waiting for transfers between devices, swap(): return lax.ppermute(array, 'vel', [(i, i ^ bits) for i in range(axis_size)])  18.2 us
    ppermute x17, starting transfers between devices, swap(): return lax.ppermute(array, 'vel', [(i, i ^ bits) for i in range(axis_size)])  18 us
    pallas_call x4, Pallas kernels, stack(): pl.pallas_call(functools.partial(stack_kernel, block, rows, sources, per_...  15.7 us
    pallas_call x1, Pallas kernels, local(): pl.pallas_call(functools.partial(window_kernel, block, chips), out_shape=...  2.81 us
    unnamed x9, local copies, waits for them, and re-layouts  2.72 us
  transfers between devices with their start and end apart: 17, of which 8 were waited for; matrix products, arithmetic and copies ran while one was open for 2% of the time, Pallas kernels for 22%

profile of v2, /device:TPU:0, one launch (start us, length us, event | category | flops | bytes accessed | tf_op | source)
XLA Modules:
  0.0 60.3 jit_solution(8635369583029948709)
XLA Ops:
  0.6 0.7 %copy.33 = s32[1,2]{0,1:T(2,128)S(1)} copy(s32[1,2]{1,0:T(1,128)} %param.6) | data formatting | bytes 16 | tf_op args[1]
  1.4 3.0 %collective-permute-start = (s32[1,2]{0,1:T(2,128)S(1)}, s32[1,2]{0,1:T(2,128)S(1)}, u32[]{:S(2)}, u32[]{:S(2)}) collective-permute-start(s32[1,2]{0,1:T(2,128)S(1)} %copy.33), channel_id=1, source_target_pairs={{0,2},{1,3},{2,0},{3,1},{4,6},{5,7},{6,4},{7,5},{8,10},{9,11},{10,... | collective-permute-start | bytes 32 | tf_op jit(solution)/shard_map/ppermute | solution.py:136
  4.3 1.6 %collective-permute-start.1 = (s32[1,2]{0,1:T(2,128)S(1)}, s32[1,2]{0,1:T(2,128)S(1)}, u32[]{:S(2)}, u32[]{:S(2)}) collective-permute-start(s32[1,2]{0,1:T(2,128)S(1)} %copy.33), channel_id=1, source_target_pairs={{0,4},{1,5},{2,6},{3,7},{4,0},{5,1},{6,2},{7,3},{8,12},{9,13},{10,... | collective-permute-start | bytes 32 | tf_op jit(solution)/shard_map/ppermute | solution.py:136
  5.9 0.0 collective-permute-start.2
  5.9 0.0 copy-start.2
  5.9 0.1 add_select_fusion
  6.0 0.6 copy-done.2
  6.6 0.0 copy-start.3
  6.6 0.2 select_reduce_fusion.1
  6.8 0.4 copy-done.3
  7.2 0.2 select_reduce_fusion
  7.4 0.1 reshape.55.time_ref
  7.5 0.0 copy-start
  7.5 2.8 %windows.1 = (bf16[176,768]{1,0:T(8,128)(2,1)}, bf16[176,768]{1,0:T(8,128)(2,1)}, bf16[176,768]{1,0:T(8,128)(2,1)}, bf16[176,768]{1,0:T(8,128)(2,1)}) custom-call(s32[1]{0:T(128)} %bitcast.place_ref, bf16[768,512]{1,0:T(8,128)(2,1)} %bitcast.20), custom_call_target="tpu_custom_call" | custom-call | tf_op jit(solution)/shard_map/windows/pallas_call | solution.py:144
  10.3 0.0 collective-permute-done
  10.3 0.0 collective-permute-done.1
  10.4 0.0 collective-permute-done.2
  10.4 0.1 pad_add_fusion.1
  10.5 3.0 %collective-permute-start.3 = (s32[4,2]{0,1:T(2,128)S(1)}, s32[4,2]{0,1:T(2,128)S(1)}, u32[]{:S(2)}, u32[]{:S(2)}) collective-permute-start(s32[4,2]{0,1:T(2,128)S(1)} %pad_add_fusion.1), channel_id=1, source_target_pairs={{0,8},{1,9},{2,10},{3,11},{4,12},{5,13},{6,14},{7,15},{8,0},{9,1},... | collective-permute-start | bytes 104 | tf_op jit(solution)/shard_map/ppermute | solution.py:136
  13.4 1.5 %collective-permute-start.6 = (bf16[176,768]{1,0:T(8,128)(2,1)}, bf16[176,768]{1,0:T(8,128)(2,1)S(1)}, u32[]{:S(2)}, u32[]{:S(2)}) collective-permute-start(bf16[176,768]{1,0:T(8,128)(2,1)} %get-tuple-element.28), channel_id=1, source_target_pairs={{0,2},{1,3},{2,0},{3,1},{4,6},{5,7},{6,4},{7,5},{8,10},{9,11},{10,... | collective-permute-start | bytes 811016 | tf_op jit(solution)/shard_map/ppermute | solution.py:136
  14.9 1.6 %collective-permute-start.7 = (bf16[176,768]{1,0:T(8,128)(2,1)}, bf16[176,768]{1,0:T(8,128)(2,1)S(1)}, u32[]{:S(2)}, u32[]{:S(2)}) collective-permute-start(bf16[176,768]{1,0:T(8,128)(2,1)} %get-tuple-element.29), channel_id=1, source_target_pairs={{0,4},{1,5},{2,6},{3,7},{4,0},{5,1},{6,2},{7,3},{8,12},{9,13},{10,... | collective-permute-start | bytes 811016 | tf_op jit(solution)/shard_map/ppermute | solution.py:136
  16.5 0.4 collective-permute-start.5
  16.9 0.0 collective-permute-done.3
  16.9 0.1 pad_add_fusion.2
  17.0 0.0 collective-permute-start.4
  17.0 0.1 fusion.14
  17.1 1.1 %collective-permute-done.4 = s32[8,2]{0,1:T(2,128)S(1)} collective-permute-done((s32[8,2]{0,1:T(2,128)S(1)}, s32[8,2]{0,1:T(2,128)S(1)}, u32[]{:S(2)}, u32[]{:S(2)}) %collective-permute-start.4) | collective-permute-done | bytes 96 | tf_op jit(solution)/shard_map/ppermute | solution.py:136
  18.1 0.1 copy.39
  18.2 0.0 copy-done
  18.2 0.0 copy-start.1
  18.2 1.0 %copy-done.1 = bf16[176,768]{1,0:T(8,128)(2,1)S(1)} copy-done((bf16[176,768]{1,0:T(8,128)(2,1)S(1)}, bf16[176,768]{1,0:T(8,128)(2,1)}, u32[]{:S(2)}) %copy-start.1) | copy-done | bytes 270360
  19.2 4.2 %stack.16 = (f32[8,96,128]{2,1,0:T(8,128)S(1)}, f32[8,96,128]{2,1,0:T(8,128)S(1)}) custom-call(s32[32]{0:T(128)S(1)} %reshape.55.time_ref, s32[16,2]{1,0:T(8,128)S(1)} %bitcast.16, bf16[96,512]{1,0:T(8,128)(2,1)S(1)} %copy-done, bf16[176,768]{1,0:T(8,128)(2,1)S(1)} %copy-done.1), custom_call_target="tpu_custom_call" | custom-call | tf_op jit(solution)/shard_map/stack/pallas_call | solution.py:171
  23.4 0.0 collective-permute-done.6.refs_0_
  23.4 1.2 %collective-permute-done.7.refs_1_ = bf16[176,768]{1,0:T(8,128)(2,1)S(1)} collective-permute-done((bf16[176,768]{1,0:T(8,128)(2,1)}, bf16[176,768]{1,0:T(8,128)(2,1)S(1)}, u32[]{:S(2)}, u32[]{:S(2)}) %collective-permute-start.7) | collective-permute-done | bytes 270368 | tf_op jit(solution)/shard_map/ppermute | solution.py:136
  24.6 6.1 %stack.17 = (f32[8,96,128]{2,1,0:T(8,128)S(1)}, f32[8,96,128]{2,1,0:T(8,128)S(1)}) custom-call(s32[32]{0:T(128)S(1)} %reshape.55.time_ref, s32[16,2]{1,0:T(8,128)S(1)} %bitcast.17, bf16[96,512]{1,0:T(8,128)(2,1)S(1)} %copy-done, bf16[176,768]{1,0:T(8,128)(2,1)S(1)} %collective-permute-done.6.refs_0_, bf16[176,768]{1,0:T(8,128)(2,1)S(1)} %collective-permute-done.7.refs_1_, ...), custom_call_target="tpu_custom_call" | custom-call | tf_op jit(solution)/shard_map/stack/pallas_call | solution.py:171
  30.7 0.1 fusion.12
  30.7 0.0 collective-permute-done.5.refs_0_
  30.7 2.7 %stack.18 = (f32[4,96,128]{2,1,0:T(8,128)S(1)}, f32[4,96,128]{2,1,0:T(8,128)S(1)}) custom-call(s32[32]{0:T(128)S(1)} %reshape.55.time_ref, s32[16,2]{1,0:T(8,128)S(1)} %bitcast.18, bf16[96,512]{1,0:T(8,128)(2,1)S(1)} %copy-done, bf16[176,768]{1,0:T(8,128)(2,1)S(1)} %collective-permute-done.5.refs_0_, f32[4,96,128]{2,1,0:T(8,128)S(1)} %get-tuple-element.62.refs_1_, ...), custom_call_target="tpu_custom_call" | custom-call | tf_op jit(solution)/shard_map/stack/pallas_call | solution.py:171
  33.4 0.1 collective-permute-start.8
  33.5 1.4 %collective-permute-done.8 = f32[4,96,128]{2,1,0:T(8,128)S(1)} collective-permute-done((f32[4,96,128]{2,1,0:T(8,128)S(1)}, f32[4,96,128]{2,1,0:T(8,128)S(1)}, u32[]{:S(2)}, u32[]{:S(2)}) %collective-permute-start.8) | collective-permute-done | bytes 196640 | tf_op jit(solution)/shard_map/ppermute | solution.py:136
  34.9 2.8 %stack.19 = (f32[4,96,128]{2,1,0:T(8,128)S(1)}, f32[4,96,128]{2,1,0:T(8,128)S(1)}) custom-call(s32[32]{0:T(128)S(1)} %reshape.55.time_ref, s32[16,2]{1,0:T(8,128)S(1)} %bitcast.19, bf16[96,512]{1,0:T(8,128)(2,1)S(1)} %copy-done, bf16[176,768]{1,0:T(8,128)(2,1)S(1)} %collective-permute-done.5.refs_0_, f32[4,96,128]{2,1,0:T(8,128)S(1)} %get-tuple-element.37.refs_1_, ...), custom_call_target="tpu_custom_call" | custom-call | tf_op jit(solution)/shard_map/stack/pallas_call | solution.py:171
  37.8 0.2 collective-permute-start.9
  38.0 0.3 collective-permute-start.10
  38.3 7.7 %collective-permute-done.10 = f16[4,96,128]{2,1,0:T(8,128)(2,1)S(1)} collective-permute-done((f16[4,96,128]{2,1,0:T(8,128)(2,1)S(1)}, f16[4,96,128]{2,1,0:T(8,128)(2,1)S(1)}, u32[]{:S(2)}, u32[]{:S(2)}) %collective-permute-start.10) | collective-permute-done | bytes 98336 | tf_op jit(solution)/shard_map/ppermute | solution.py:136
  46.1 0.0 collective-permute-done.9
  46.1 0.1 fusion.10
  46.1 0.1 collective-permute-start.11
  46.2 0.1 collective-permute-start.12
  46.3 2.7 %collective-permute-start.13 = (f32[96,128]{1,0:T(8,128)S(1)}, f32[96,128]{1,0:T(8,128)S(1)}, u32[]{:S(2)}, u32[]{:S(2)}) collective-permute-start(f32[96,128]{1,0:T(8,128)S(1)} %get-tuple-element.44), channel_id=1, source_target_pairs={{0,9},{1,8},{2,11},{3,10},{4,13},{5,12},{6,15},{7,14},{8,1},{9,0},... | collective-permute-start | bytes 147464 | tf_op jit(solution)/shard_map/ppermute | solution.py:136
  49.0 0.0 collective-permute-done.11
  49.0 3.8 %collective-permute-done.12 = f32[96,128]{1,0:T(8,128)S(1)} collective-permute-done((f32[96,128]{1,0:T(8,128)S(1)}, f32[96,128]{1,0:T(8,128)S(1)}, u32[]{:S(2)}, u32[]{:S(2)}) %collective-permute-start.12) | collective-permute-done | bytes 49184 | tf_op jit(solution)/shard_map/ppermute | solution.py:136
  52.8 0.3 collective-permute-done.13
  53.1 0.2 collective-permute-start.14
  53.3 1.9 %collective-permute-start.15 = (f16[192,128]{1,0:T(8,128)(2,1)S(1)}, f16[192,128]{1,0:T(8,128)(2,1)S(1)}, u32[]{:S(2)}, u32[]{:S(2)}) collective-permute-start(f16[192,128]{1,0:T(8,128)(2,1)S(1)} %get-tuple-element.60), channel_id=1, source_target_pairs={{0,4},{1,5},{2,6},{3,7},{4,0},{5,1},{6,2},{7,3},{8,12},{9,13},{10,... | collective-permute-start | bytes 147464 | tf_op jit(solution)/shard_map/ppermute | solution.py:136
  55.2 1.5 %collective-permute-start.16 = (f16[192,128]{1,0:T(8,128)(2,1)S(1)}, f16[192,128]{1,0:T(8,128)(2,1)S(1)}, u32[]{:S(2)}, u32[]{:S(2)}) collective-permute-start(f16[192,128]{1,0:T(8,128)(2,1)S(1)} %get-tuple-element.59), channel_id=1, source_target_pairs={{0,2},{1,3},{2,0},{3,1},{4,6},{5,7},{6,4},{7,5},{8,10},{9,11},{10,... | collective-permute-start | bytes 147464 | tf_op jit(solution)/shard_map/ppermute | solution.py:136
  56.7 1.8 %collective-permute-done.14 = f16[192,128]{1,0:T(8,128)(2,1)S(1)} collective-permute-done((f16[192,128]{1,0:T(8,128)(2,1)S(1)}, f16[192,128]{1,0:T(8,128)(2,1)S(1)}, u32[]{:S(2)}, u32[]{:S(2)}) %collective-permute-start.14) | collective-permute-done | bytes 49184 | tf_op jit(solution)/shard_map/ppermute | solution.py:136
  58.5 0.0 collective-permute-done.15
  58.5 0.8 %collective-permute-done.16 = f16[192,128]{1,0:T(8,128)(2,1)S(1)} collective-permute-done((f16[192,128]{1,0:T(8,128)(2,1)S(1)}, f16[192,128]{1,0:T(8,128)(2,1)S(1)}, u32[]{:S(2)}, u32[]{:S(2)}) %collective-permute-start.16) | collective-permute-done | bytes 49184 | tf_op jit(solution)/shard_map/ppermute | solution.py:136
  59.4 0.1 broadcast_select_fusion.6
  59.4 0.1 convert_multiply_fusion
  59.5 0.8 %fusion.11 = (f32[96,512]{1,0:T(8,128)}, f32[1,96,512]{2,1,0:T(8,128)}) fusion(f32[192,512]{1,0:T(8,128)S(1)} %convert_multiply_fusion), kind=kLoop, calls=%fused_computation.42 | loop fusion | bytes 786432 | tf_op jit(solution)/shard_map/slice | solution.py:207
  (7 shorter events, 0.1 us)
Async XLA Ops:
  1.4 9.0 %collective-permute-start = (s32[1,2]{0,1:T(2,128)S(1)}, s32[1,2]{0,1:T(2,128)S(1)}, u32[]{:S(2)}, u32[]{:S(2)}) collective-permute-start(s32[1,2]{0,1:T(2,128)S(1)} %copy.33), channel_id=1, source_target_pairs={{0,2},{1,3},{2,0},{3,1},{4,6},{5,7},{6,4},{7,5},{8,10},{9,11},{10,... | collective-permute-start | bytes 32 | tf_op jit(solution)/shard_map/ppermute | solution.py:136
  4.3 6.0 %collective-permute-start.1 = (s32[1,2]{0,1:T(2,128)S(1)}, s32[1,2]{0,1:T(2,128)S(1)}, u32[]{:S(2)}, u32[]{:S(2)}) collective-permute-start(s32[1,2]{0,1:T(2,128)S(1)} %copy.33), channel_id=1, source_target_pairs={{0,4},{1,5},{2,6},{3,7},{4,0},{5,1},{6,2},{7,3},{8,12},{9,13},{10,... | collective-permute-start | bytes 32 | tf_op jit(solution)/shard_map/ppermute | solution.py:136
  5.9 4.5 %collective-permute-start.2 = (s32[1,2]{0,1:T(2,128)S(1)}, s32[1,2]{0,1:T(2,128)S(1)}, u32[]{:S(2)}, u32[]{:S(2)}) collective-permute-start(s32[1,2]{0,1:T(2,128)S(1)} %copy.33), channel_id=1, source_target_pairs={{0,6},{1,7},{2,4},{3,5},{4,2},{5,3},{6,0},{7,1},{8,14},{9,15},{10,... | collective-permute-start | bytes 32 | tf_op jit(solution)/shard_map/ppermute | solution.py:136
  5.9 0.7 %copy-start.2 = (s32[64]{0:T(128)S(1)}, s32[64]{0:T(128)}, u32[]{:S(2)}) copy-start(s32[64]{0:T(128)} %param.7) | copy-start | bytes 772
  6.6 0.7 %copy-start.3 = (s32[64]{0:T(128)S(1)}, s32[64]{0:T(128)}, u32[]{:S(2)}) copy-start(s32[64]{0:T(128)} %param.8) | copy-start | bytes 772
  7.5 10.7 %copy-start = (bf16[96,512]{1,0:T(8,128)(2,1)S(1)}, bf16[96,512]{1,0:T(8,128)(2,1)}, u32[]{:S(2)}) copy-start(bf16[96,512]{1,0:T(8,128)(2,1)} %constant.60.clone.filter_ref) | copy-start | bytes 294916
  10.5 6.5 %collective-permute-start.3 = (s32[4,2]{0,1:T(2,128)S(1)}, s32[4,2]{0,1:T(2,128)S(1)}, u32[]{:S(2)}, u32[]{:S(2)}) collective-permute-start(s32[4,2]{0,1:T(2,128)S(1)} %pad_add_fusion.1), channel_id=1, source_target_pairs={{0,8},{1,9},{2,10},{3,11},{4,12},{5,13},{6,14},{7,15},{8,0},{9,1},... | collective-permute-start | bytes 104 | tf_op jit(solution)/shard_map/ppermute | solution.py:136
  13.4 9.9 %collective-permute-start.6 = (bf16[176,768]{1,0:T(8,128)(2,1)}, bf16[176,768]{1,0:T(8,128)(2,1)S(1)}, u32[]{:S(2)}, u32[]{:S(2)}) collective-permute-start(bf16[176,768]{1,0:T(8,128)(2,1)} %get-tuple-element.28), channel_id=1, source_target_pairs={{0,2},{1,3},{2,0},{3,1},{4,6},{5,7},{6,4},{7,5},{8,10},{9,11},{10,... | collective-permute-start | bytes 811016 | tf_op jit(solution)/shard_map/ppermute | solution.py:136
  14.9 9.6 %collective-permute-start.7 = (bf16[176,768]{1,0:T(8,128)(2,1)}, bf16[176,768]{1,0:T(8,128)(2,1)S(1)}, u32[]{:S(2)}, u32[]{:S(2)}) collective-permute-start(bf16[176,768]{1,0:T(8,128)(2,1)} %get-tuple-element.29), channel_id=1, source_target_pairs={{0,4},{1,5},{2,6},{3,7},{4,0},{5,1},{6,2},{7,3},{8,12},{9,13},{10,... | collective-permute-start | bytes 811016 | tf_op jit(solution)/shard_map/ppermute | solution.py:136
  16.5 14.2 %collective-permute-start.5 = (bf16[176,768]{1,0:T(8,128)(2,1)}, bf16[176,768]{1,0:T(8,128)(2,1)S(1)}, u32[]{:S(2)}, u32[]{:S(2)}) collective-permute-start(bf16[176,768]{1,0:T(8,128)(2,1)} %get-tuple-element.27), channel_id=1, source_target_pairs={{0,6},{1,7},{2,4},{3,5},{4,2},{5,3},{6,0},{7,1},{8,14},{9,15},{10,... | collective-permute-start | bytes 811016 | tf_op jit(solution)/shard_map/ppermute | solution.py:136
  17.0 1.1 %collective-permute-start.4 = (s32[8,2]{0,1:T(2,128)S(1)}, s32[8,2]{0,1:T(2,128)S(1)}, u32[]{:S(2)}, u32[]{:S(2)}) collective-permute-start(s32[8,2]{0,1:T(2,128)S(1)} %pad_add_fusion.2), channel_id=1, source_target_pairs={{0,1},{1,0},{2,3},{3,2},{4,5},{5,4},{6,7},{7,6},{8,9},{9,8},{10,11... | collective-permute-start | bytes 200 | tf_op jit(solution)/shard_map/ppermute | solution.py:136
  18.2 1.0 %copy-start.1 = (bf16[176,768]{1,0:T(8,128)(2,1)S(1)}, bf16[176,768]{1,0:T(8,128)(2,1)}, u32[]{:S(2)}) copy-start(bf16[176,768]{1,0:T(8,128)(2,1)} %get-tuple-element.30.refs_0_) | copy-start | bytes 811012
  33.4 1.5 %collective-permute-start.8 = (f32[4,96,128]{2,1,0:T(8,128)S(1)}, f32[4,96,128]{2,1,0:T(8,128)S(1)}, u32[]{:S(2)}, u32[]{:S(2)}) collective-permute-start(f32[4,96,128]{2,1,0:T(8,128)S(1)} %get-tuple-element.36), channel_id=1, source_target_pairs={{0,1},{1,0},{2,3},{3,2},{4,5},{5,4},{6,7},{7,6},{8,9},{9,8},{10,11... | collective-permute-start | bytes 589832 | tf_op jit(solution)/shard_map/ppermute | solution.py:136
  37.8 8.3 %collective-permute-start.9 = (f32[4,96,128]{2,1,0:T(8,128)S(1)}, f32[4,96,128]{2,1,0:T(8,128)S(1)}, u32[]{:S(2)}, u32[]{:S(2)}) collective-permute-start(f32[4,96,128]{2,1,0:T(8,128)S(1)} %get-tuple-element.40), channel_id=1, source_target_pairs={{0,1},{1,0},{2,3},{3,2},{4,5},{5,4},{6,7},{7,6},{8,9},{9,8},{10,11... | collective-permute-start | bytes 589832 | tf_op jit(solution)/shard_map/ppermute | solution.py:136
  38.0 8.1 %collective-permute-start.10 = (f16[4,96,128]{2,1,0:T(8,128)(2,1)S(1)}, f16[4,96,128]{2,1,0:T(8,128)(2,1)S(1)}, u32[]{:S(2)}, u32[]{:S(2)}) collective-permute-start(f16[4,96,128]{2,1,0:T(8,128)(2,1)S(1)} %add_convert_fusion), channel_id=1, source_target_pairs={{0,8},{1,9},{2,10},{3,11},{4,12},{5,13},{6,14},{7,15},{8,0},{9,1},... | collective-permute-start | bytes 294920 | tf_op jit(solution)/shard_map/ppermute | solution.py:136
  46.1 2.9 %collective-permute-start.11 = (f32[96,128]{1,0:T(8,128)S(1)}, f32[96,128]{1,0:T(8,128)S(1)}, u32[]{:S(2)}, u32[]{:S(2)}) collective-permute-start(f32[96,128]{1,0:T(8,128)S(1)} %get-tuple-element.44), channel_id=1, source_target_pairs={{0,1},{1,0},{2,3},{3,2},{4,5},{5,4},{6,7},{7,6},{8,9},{9,8},{10,11... | collective-permute-start | bytes 147464 | tf_op jit(solution)/shard_map/ppermute | solution.py:136
  46.2 6.6 %collective-permute-start.12 = (f32[96,128]{1,0:T(8,128)S(1)}, f32[96,128]{1,0:T(8,128)S(1)}, u32[]{:S(2)}, u32[]{:S(2)}) collective-permute-start(f32[96,128]{1,0:T(8,128)S(1)} %get-tuple-element.44), channel_id=1, source_target_pairs={{0,8},{1,9},{2,10},{3,11},{4,12},{5,13},{6,14},{7,15},{8,0},{9,1},... | collective-permute-start | bytes 147464 | tf_op jit(solution)/shard_map/ppermute | solution.py:136
  46.3 6.8 %collective-permute-start.13 = (f32[96,128]{1,0:T(8,128)S(1)}, f32[96,128]{1,0:T(8,128)S(1)}, u32[]{:S(2)}, u32[]{:S(2)}) collective-permute-start(f32[96,128]{1,0:T(8,128)S(1)} %get-tuple-element.44), channel_id=1, source_target_pairs={{0,9},{1,8},{2,11},{3,10},{4,13},{5,12},{6,15},{7,14},{8,1},{9,0},... | collective-permute-start | bytes 147464 | tf_op jit(solution)/shard_map/ppermute | solution.py:136
  53.1 5.3 %collective-permute-start.14 = (f16[192,128]{1,0:T(8,128)(2,1)S(1)}, f16[192,128]{1,0:T(8,128)(2,1)S(1)}, u32[]{:S(2)}, u32[]{:S(2)}) collective-permute-start(f16[192,128]{1,0:T(8,128)(2,1)S(1)} %get-tuple-element.61), channel_id=1, source_target_pairs={{0,6},{1,7},{2,4},{3,5},{4,2},{5,3},{6,0},{7,1},{8,14},{9,15},{10,... | collective-permute-start | bytes 147464 | tf_op jit(solution)/shard_map/ppermute | solution.py:136
  53.3 5.2 %collective-permute-start.15 = (f16[192,128]{1,0:T(8,128)(2,1)S(1)}, f16[192,128]{1,0:T(8,128)(2,1)S(1)}, u32[]{:S(2)}, u32[]{:S(2)}) collective-permute-start(f16[192,128]{1,0:T(8,128)(2,1)S(1)} %get-tuple-element.60), channel_id=1, source_target_pairs={{0,4},{1,5},{2,6},{3,7},{4,0},{5,1},{6,2},{7,3},{8,12},{9,13},{10,... | collective-permute-start | bytes 147464 | tf_op jit(solution)/shard_map/ppermute | solution.py:136
  55.2 4.1 %collective-permute-start.16 = (f16[192,128]{1,0:T(8,128)(2,1)S(1)}, f16[192,128]{1,0:T(8,128)(2,1)S(1)}, u32[]{:S(2)}, u32[]{:S(2)}) collective-permute-start(f16[192,128]{1,0:T(8,128)(2,1)S(1)} %get-tuple-element.59), channel_id=1, source_target_pairs={{0,2},{1,3},{2,0},{3,1},{4,6},{5,7},{6,4},{7,5},{8,10},{9,11},{10,... | collective-permute-start | bytes 147464 | tf_op jit(solution)/shard_map/ppermute | solution.py:136

commit v3 on v2

v3 whole, which is shorter than its diff:
```python
import functools

import jax
import jax.numpy as jnp
import ml_dtypes
import numpy as np
from jax import lax
from jax.experimental import pallas as pl
from jax.experimental.pallas import tpu as pltpu
from jax.sharding import PartitionSpec as P

SPLINE = np.array(
    [
        [64.0, 256.0, 64.0, 0.0],
        [27.0, 235.0, 121.0, 1.0],
        [8.0, 184.0, 184.0, 8.0],
        [1.0, 121.0, 235.0, 27.0],
    ],
    np.float32,
)
spline_norm = 147456.0
rate_divisor = 32
HALO = 24
LANES = 128
PACK = 16
LINK_SCALE = 64.0


def row_filter(rows):
    band = np.zeros((rows, 4 * LANES), np.float32)
    for row in range(rows):
        for tap in range(4):
            for fraction in range(4):
                band[row, fraction * LANES + (row - tap + 1) % LANES] = SPLINE[fraction, tap]
    return band.astype(ml_dtypes.bfloat16)


def window_kernel(block, per_device, device_ref, slot_ref, epoch_time_ref, image_ref, time_ref, *refs):
    *window_refs, padded = refs
    chips = len(window_refs)
    epochs = slot_ref.shape[0]
    place = (device_ref[0] >> 1) & (chips - 1)
    for relative in range(chips):
        source = device_ref[0] ^ (2 * relative)
        for number in range(per_device):
            slot = lax.rem(source * per_device + number, epochs)
            time_ref[relative * per_device + number] = epoch_time_ref[slot_ref[slot]]
    lanes, columns = image_ref.shape
    image = jnp.concatenate([image_ref[...], jnp.zeros((lanes, LANES), image_ref.dtype)], axis=1)
    image = pltpu.roll(image, HALO, 1)
    for first in range(0, columns + LANES, LANES):
        padded[first : first + LANES] = image[:, first : first + LANES].T
    for relative, window_ref in enumerate(window_refs):
        start = pl.multiple_of((place ^ relative) * block, block)
        window_ref[...] = padded[pl.ds(start, block + 2 * HALO)]


def stack_kernel(block, rows, sources, images, first, scale, fresh, carried, time_ref, rate_ref, filter_ref, *refs):
    count = len(sources)
    given, before, refs = refs[:count], refs[count:][:carried], refs[count + carried :]
    keep_ref, send_ref, *refs = refs
    kept, refs = (refs[:count], refs[count:]) if fresh else (given, refs)
    bands, own, times, rates, semaphores, *bins = refs
    fetches = [
        pltpu.make_async_copy(time_ref, times, semaphores.at[0]),
        pltpu.make_async_copy(rate_ref, rates, semaphores.at[1]),
    ]
    for fetch in fetches:
        fetch.start()
    if fresh and sources[0] == 0:
        copy = pltpu.make_async_copy(given[0], own, semaphores.at[2])
        copy.start()
    together = len(bins)
    turns = bins[0].shape[0] // 4
    reach = bins[0].shape[1] - PACK
    wide = block + 2 * HALO
    lanes = images * rows
    offsets = sorted({rows * number % LANES for number in range(images)})
    if fresh:
        bands[...] = jnp.zeros(bands.shape, bands.dtype)
        for number, offset in enumerate(offsets):
            bands[number, offset : offset + rows] = filter_ref[...]
        for filtered in kept:
            if filtered.shape[2] > wide:
                filtered[:, :, wide:] = jnp.zeros((*filtered.shape[:2], filtered.shape[2] - wide, LANES), filtered.dtype)
    for part in bins:
        part[...] = jnp.zeros(part.shape, part.dtype)
    for index, relative in enumerate(sources):
        filtered, window_ref = kept[index], given[index]
        if fresh and relative == 0:
            copy.wait()
            window_ref = own
        for number in range(images):
            if fresh:
                low = rows * number // LANES * LANES
                high = min(lanes, (rows * (number + 1) + LANES - 1) // LANES * LANES)
                band = bands[offsets.index(rows * number - low), : high - low]
                product = jnp.dot(window_ref[:, low:high], band, preferred_element_type=jnp.float32)
                product = product.astype(jnp.bfloat16)
                for fraction in range(4):
                    filtered[number, fraction, :wide] = product[:, fraction * LANES : (fraction + 1) * LANES]
            if index == 0 and number == 0:
                for fetch in fetches:
                    fetch.wait()
            time = times[relative * images + number]

            def add(turn, _, time=time, number=number, filtered=filtered):
                for lane in range(together):
                    v = first + turn * together + lane
                    rate = (v & 1) * (rates.shape[0] // 2) + (v >> 1) * 2
                    row_offset = (rates[rate] * time) >> 5
                    column_offset = (rates[rate + 1] * time) >> 5
                    start = HALO - 1 + (column_offset >> 2)
                    even = pl.multiple_of((start >> 4) << 4, PACK)
                    shifted = filtered[number, row_offset & 3, pl.ds(even, reach), :]
                    shifted = pltpu.roll(shifted, (LANES - (row_offset >> 2)) & (LANES - 1), 1)
                    place = 4 * turn + (column_offset & 3)
                    bins[lane][place, pl.ds(PACK - (start - even), reach), :] += shifted.astype(jnp.float32)
                return _

            if turns == 1:
                add(0, 0)
            else:
                lax.fori_loop(0, turns, add, 0)

    def finish(turn, _):
        for lane in range(together):
            v = turn * together + lane
            total = jnp.zeros((block, LANES), jnp.float32)
            for fraction in range(4):
                for tap in range(4):
                    if SPLINE[fraction, tap]:
                        taken = bins[lane][4 * turn + fraction, PACK + tap : PACK + tap + block, :]
                        total = total + float(SPLINE[fraction, tap]) * taken
            total = (total * scale).T[:rows]
            if before:
                total = total + before[lane & 1][v >> 1]
            (send_ref if lane & 1 else keep_ref)[v >> 1] = total
        return _

    if turns == 1:
        finish(0, 0)
    else:
        lax.fori_loop(0, turns, finish, 0)


def arrange(pieces, place):
    step = 1
    while step < len(pieces):
        flip = (place & step) != 0
        pieces = [jnp.where(flip, pieces[x ^ step], pieces[x]) for x in range(len(pieces))]
        step *= 2
    return jnp.concatenate(pieces, axis=-1)


def local(axis_size, epoch_maps, velocity, slot_epoch, epoch_time):
    per_device, rows, columns = epoch_maps.shape
    epochs = slot_epoch.shape[0]
    half = axis_size // 2
    chips = half // 2
    block = columns // chips
    device = lax.axis_index("vel").astype(jnp.int32)
    place = device % half // 2

    def swap(array, bits):
        return lax.ppermute(array, "vel", [(i, i ^ bits) for i in range(axis_size)])

    smem = pl.BlockSpec(memory_space=pltpu.SMEM)
    vmem = pl.BlockSpec(memory_space=pltpu.VMEM)
    hbm = pl.BlockSpec(memory_space=pltpu.HBM)
    lanes = per_device * rows
    wide = block + 2 * HALO
    shape = jax.ShapeDtypeStruct

    def cost(microseconds):
        return pl.CostEstimate(flops=microseconds * 10**9, bytes_accessed=microseconds * 3 * 10**6, transcendentals=0)


    rates = velocity.reshape(-1)
    rates = jnp.concatenate([rates] + [swap(rates, 2 * x) for x in range(1, chips)])
    times, *windows = pl.pallas_call(
        functools.partial(window_kernel, block, per_device),
        out_shape=[shape((chips * per_device,), jnp.int32)] + [shape((wide, lanes), epoch_maps.dtype)] * chips,
        in_specs=[smem] * 3 + [vmem],
        out_specs=[smem] + [vmem] * chips,
        scratch_shapes=[pltpu.VMEM((columns + LANES, lanes), epoch_maps.dtype)],
        compiler_params=pltpu.CompilerParams(vmem_limit_bytes=16 * 1024 * 1024),
        cost_estimate=cost(3),
        name="windows",
    )(device.reshape(1), slot_epoch, epoch_time, epoch_maps.reshape(lanes, columns))

    windows[2:], rates = lax.optimization_barrier((windows[2:], rates))
    rates = jnp.concatenate([rates, swap(rates, half)])
    rates = jnp.concatenate([rates, swap(rates, 1)])
    windows = [windows[0]] + [swap(windows[x], 2 * x) for x in range(1, chips)]

    reach = (block + 2 + PACK + PACK - 1) // PACK * PACK
    band = jnp.asarray(row_filter(rows))

    tall = max(wide, 2 * PACK + reach)

    def stack(sources, first, count, given, carried=(), fresh=True):
        together = min(count, 16)
        filtered = shape((per_device, 4, tall, LANES), jnp.bfloat16)
        keep, send, *filtered = pl.pallas_call(
            functools.partial(
                stack_kernel,
                *(block, rows, sources, per_device, first, LINK_SCALE / spline_norm, fresh, len(carried)),
            ),
            out_shape=[shape((count // 2, rows, block), jnp.float32)] * 2 + [filtered] * (fresh * len(sources)),
            in_specs=[hbm, hbm, vmem]
            + [hbm if x == 0 and fresh else vmem for x in sources]
            + [vmem] * len(carried),
            out_specs=[vmem] * (2 + fresh * len(sources)),
            scratch_shapes=[
                pltpu.VMEM((4, 2 * LANES, 4 * LANES), jnp.bfloat16),
                pltpu.VMEM((wide, lanes), jnp.bfloat16),
                pltpu.SMEM(times.shape, jnp.int32),
                pltpu.SMEM(rates.shape, jnp.int32),
                pltpu.SemaphoreType.DMA((3,)),
            ]
            + [pltpu.VMEM((4 * count // together, reach + PACK, LANES), jnp.float32)] * together,
            compiler_params=pltpu.CompilerParams(vmem_limit_bytes=32 * 1024 * 1024),
            cost_estimate=cost(5),
            name="stack",
        )(times, rates, band, *given, *carried)
        return keep, send, filtered

    late = [chips - 1]
    early = [x for x in range(1, chips) if x not in late]
    keep, send, _ = stack([0], 0, axis_size, windows[:1])
    far, early_rows = (keep[chips:], send[chips:]), []
    if early:
        *far, early_rows = stack(early, half, half, [windows[x] for x in early], far)
    keep_far, send_far, late_rows = stack(late, half, half, [windows[x] for x in late], far)
    far = keep_far + swap(send_far.astype(jnp.float16), 1).astype(jnp.float32)
    far = far.astype(jnp.float16)
    far, near = lax.optimization_barrier((far, (keep[:chips], send[:chips])))
    other = swap(far, half).astype(jnp.float32) * (1.0 / LINK_SCALE)
    keep_near, send_near, _ = stack(early + late, 0, half, early_rows + late_rows, near, fresh=False)
    send_near, other = lax.optimization_barrier((send_near.astype(jnp.float16), other))
    near = (keep_near + swap(send_near, 1).astype(jnp.float32)) * (1.0 / LINK_SCALE)
    first = device < half
    near = jnp.where(first, near, other) / jnp.sqrt(jnp.where(first, other, near) + 1.0)
    near = (near * LINK_SCALE).astype(jnp.float16)
    best = jnp.max(near, axis=0)
    best = jnp.maximum(jnp.maximum(best, swap(best, 1)), jnp.maximum(swap(best, half), swap(best, half + 1)))

    pieces = [jnp.concatenate([near[x], best]) for x in range(chips)]
    pieces = [pieces[0]] + [swap(pieces[x], 2 * x) for x in range(1, chips)]
    whole = arrange(pieces, place).astype(jnp.float32) * (1.0 / LINK_SCALE)
    return whole[None, :rows], whole[rows:]


def solution(mesh):
    return jax.shard_map(
        functools.partial(local, mesh.shape["vel"]),
        mesh=mesh,
        in_specs=(P("vel", "groups", None), P("vel", None), P(), P()),
        out_specs=(P("vel", "groups", None), P("groups", None)),
        check_vma=False,
    )
```

time: 60.5 us -> 53.1 us (0.88)
  waiting for transfers between devices: 18.2 us -> 12.6 us
  Pallas kernels: 18.5 us -> 14.8 us
  starting transfers between devices: 18 us -> 20.8 us
    ppermute x17, waiting for transfers between devices: 18.2 us -> 12.6 us  [swap(): return lax.ppermute(array, 'vel', [(i, i ^ bits) for i in range(axis_size)])]
    pallas_call x5, Pallas kernels: 18.5 us -> 14.8 us  [the longest x4 13 us: stack(): pl.pallas_call(functools.partial(stack_kernel, *(block, rows, sources, pe...]
    ppermute x17, starting transfers between devices: 18 us -> 20.8 us  [swap(): return lax.ppermute(array, 'vel', [(i, i ^ bits) for i in range(axis_size)])]
    unnamed x9 -> x10, local copies, waits for them, and re-layouts: 2.72 us -> 2.45 us
  transfers between devices with their start and end apart: 17 -> 17, of which waited for: 8 -> 11; matrix products, arithmetic and copies ran while one was open for 2% -> 1% of each run, Pallas kernels for 22% -> 24%
where the time goes in v3:
time: 53.1 us; the launch traced here: 52.9 us
  starting transfers between devices  20.8 us (39%)
  Pallas kernels  14.8 us (28%)
  waiting for transfers between devices  12.6 us (24%)
  local copies, waits for them, and re-layouts  3.29 us (6%)
  between operations  0.8 us (2%)
  other arithmetic  0.58 us (1%)
    ppermute x17, starting transfers between devices, swap(): return lax.ppermute(array, 'vel', [(i, i ^ bits) for i in range(axis_size)])  20.8 us
    pallas_call x4, Pallas kernels, stack(): pl.pallas_call(functools.partial(stack_kernel, *(block, rows, sources, pe...  13 us
    ppermute x17, waiting for transfers between devices, swap(): return lax.ppermute(array, 'vel', [(i, i ^ bits) for i in range(axis_size)])  12.6 us
    unnamed x10, local copies, waits for them, and re-layouts  2.45 us
    pallas_call x1, Pallas kernels, local(): pl.pallas_call(functools.partial(window_kernel, block, per_device), out_s...  1.8 us
  transfers between devices with their start and end apart: 17, of which 11 were waited for; matrix products, arithmetic and copies ran while one was open for 1% of the time, Pallas kernels for 24%

profile of v3, /device:TPU:0, one launch (start us, length us, event | category | flops | bytes accessed | tf_op | source)
XLA Modules:
  0.0 52.9 jit_solution(2189596319235159644)
XLA Ops:
  0.6 3.0 %collective-permute-start = (s32[2]{0:T(128)}, s32[2]{0:T(128)S(1)}, u32[]{:S(2)}, u32[]{:S(2)}) collective-permute-start(s32[2]{0:T(128)} %bitcast.14), channel_id=1, source_target_pairs={{0,2},{1,3},{2,0},{3,1},{4,6},{5,7},{6,4},{7,5},{8,10},{9,11},{10,... | collective-permute-start | bytes 32 | tf_op jit(solution)/shard_map/ppermute | solution.py:166
  3.7 1.6 %collective-permute-start.1 = (s32[2]{0:T(128)}, s32[2]{0:T(128)S(1)}, u32[]{:S(2)}, u32[]{:S(2)}) collective-permute-start(s32[2]{0:T(128)} %bitcast.15), channel_id=1, source_target_pairs={{0,4},{1,5},{2,6},{3,7},{4,0},{5,1},{6,2},{7,3},{8,12},{9,13},{10,... | collective-permute-start | bytes 32 | tf_op jit(solution)/shard_map/ppermute | solution.py:166
  5.2 0.0 collective-permute-start.2
  5.2 0.0 copy-start
  5.2 1.1 %copy-done = bf16[8,96,512]{2,1,0:T(8,128)(2,1)S(1)} copy-done((bf16[8,96,512]{2,1,0:T(8,128)(2,1)S(1)}, bf16[8,96,512]{2,1,0:T(8,128)(2,1)}, u32[]{:S(2)}) %copy-start) | copy-done | bytes 786456
  6.4 0.0 copy-start.1
  6.4 0.7 %copy-done.1 = s32[64]{0:T(128)S(1)} copy-done((s32[64]{0:T(128)S(1)}, s32[64]{0:T(128)}, u32[]{:S(2)}) %copy-start.1) | copy-done | bytes 280
  7.0 0.0 copy-start.2
  7.0 0.7 %copy-done.2 = s32[64]{0:T(128)S(1)} copy-done((s32[64]{0:T(128)S(1)}, s32[64]{0:T(128)}, u32[]{:S(2)}) %copy-start.2) | copy-done | bytes 280
  7.7 0.0 copy-start.4
  7.7 0.0 copy-start.3
  7.7 1.8 %windows.1 = (s32[32]{0:T(128)S(1)}, bf16[176,768]{1,0:T(8,128)(2,1)S(1)}, bf16[176,768]{1,0:T(8,128)(2,1)S(1)}, bf16[176,768]{1,0:T(8,128)(2,1)S(1)}, bf16[176,768]{1,0:T(8,128)(2,1)S(1)}) custom-call(s32[1]{0:T(128)} %bitcast.device_ref, s32[64]{0:T(128)S(1)} %copy-done.1, s32[64]{0:T(128)S(1)} %copy-done.2, bf16[768,512]{1,0:T(8,128)(2,1)S(1)} %bitcast.13), custom_call_target="tpu_custom_call" | custom-call | flops 3000000000 | bytes 9000000 | tf_op jit(solution)/shard_map/windows/pallas_call | solution.py:181
  9.5 2.0 %collective-permute-start.5 = (bf16[176,768]{1,0:T(8,128)(2,1)S(1)}, bf16[176,768]{1,0:T(8,128)(2,1)S(1)}, u32[]{:S(2)}, u32[]{:S(2)}) collective-permute-start(bf16[176,768]{1,0:T(8,128)(2,1)S(1)} %get-tuple-element.30), channel_id=1, source_target_pairs={{0,2},{1,3},{2,0},{3,1},{4,6},{5,7},{6,4},{7,5},{8,10},{9,11},{10,... | collective-permute-start | bytes 811016 | tf_op jit(solution)/shard_map/ppermute | solution.py:166
  11.5 0.0 collective-permute-done
  11.5 0.0 collective-permute-done.1
  11.5 0.0 collective-permute-done.2
  11.5 0.0 copy-done.4
  11.5 0.1 pad_add_fusion
  11.6 2.6 %collective-permute-start.3 = (s32[8]{0:T(128)S(1)}, s32[8]{0:T(128)S(1)}, u32[]{:S(2)}, u32[]{:S(2)}) collective-permute-start(s32[8]{0:T(128)S(1)} %pad_add_fusion), channel_id=1, source_target_pairs={{0,8},{1,9},{2,10},{3,11},{4,12},{5,13},{6,14},{7,15},{8,0},{9,1},... | collective-permute-start | bytes 104 | tf_op jit(solution)/shard_map/ppermute | solution.py:166
  14.2 1.6 %collective-permute-start.6 = (bf16[176,768]{1,0:T(8,128)(2,1)S(1)}, bf16[176,768]{1,0:T(8,128)(2,1)S(1)}, u32[]{:S(2)}, u32[]{:S(2)}) collective-permute-start(bf16[176,768]{1,0:T(8,128)(2,1)S(1)} %get-tuple-element.31), channel_id=1, source_target_pairs={{0,4},{1,5},{2,6},{3,7},{4,0},{5,1},{6,2},{7,3},{8,12},{9,13},{10,... | collective-permute-start | bytes 811016 | tf_op jit(solution)/shard_map/ppermute | solution.py:166
  15.8 0.3 collective-permute-done.3
  16.0 0.1 pad_add_fusion.1
  16.1 0.0 collective-permute-start.4
  16.1 1.6 %collective-permute-start.7 = (bf16[176,768]{1,0:T(8,128)(2,1)S(1)}, bf16[176,768]{1,0:T(8,128)(2,1)S(1)}, u32[]{:S(2)}, u32[]{:S(2)}) collective-permute-start(bf16[176,768]{1,0:T(8,128)(2,1)S(1)} %get-tuple-element.37), channel_id=1, source_target_pairs={{0,6},{1,7},{2,4},{3,5},{4,2},{5,3},{6,0},{7,1},{8,14},{9,15},{10,... | collective-permute-start | bytes 811016 | tf_op jit(solution)/shard_map/ppermute | solution.py:166
  17.8 0.0 collective-permute-done.4
  17.8 0.1 pad_add_fusion.2.rate_ref
  17.8 0.0 copy-done.3
  17.8 3.9 %stack.4 = (f32[8,96,128]{2,1,0:T(8,128)S(1)}, f32[8,96,128]{2,1,0:T(8,128)S(1)}, bf16[8,4,192,128]{3,2,1,0:T(8,128)(2,1)}) custom-call(s32[32]{0:T(128)S(1)} %get-tuple-element.26.time_ref, s32[32]{0:T(128)S(1)} %pad_add_fusion.2.rate_ref, bf16[96,512]{1,0:T(8,128)(2,1)S(1)} %copy-done.3, bf16[176,768]{1,0:T(8,128)(2,1)S(1)} %get-tuple-element.32.refs_0_), custom_call_target="tpu_custom_call" | custom-call | flops 5000000000 | bytes 15000000 | tf_op jit(solution)/shard_map/stack/pallas_call | solution.py:205
  21.7 0.1 fusion.2
  21.8 0.0 collective-permute-done.5.refs_0_
  21.8 1.0 %collective-permute-done.6.refs_1_ = bf16[176,768]{1,0:T(8,128)(2,1)S(1)} collective-permute-done((bf16[176,768]{1,0:T(8,128)(2,1)S(1)}, bf16[176,768]{1,0:T(8,128)(2,1)S(1)}, u32[]{:S(2)}, u32[]{:S(2)}) %collective-permute-start.6) | collective-permute-done | bytes 270368 | tf_op jit(solution)/shard_map/ppermute | solution.py:166
  22.8 3.4 %stack.5 = (f32[4,96,128]{2,1,0:T(8,128)S(1)}, f32[4,96,128]{2,1,0:T(8,128)S(1)}, bf16[8,4,192,128]{3,2,1,0:T(8,128)(2,1)S(1)}, bf16[8,4,192,128]{3,2,1,0:T(8,128)(2,1)S(1)}) custom-call(s32[32]{0:T(128)S(1)} %get-tuple-element.26.time_ref, s32[32]{0:T(128)S(1)} %pad_add_fusion.2.rate_ref, bf16[96,512]{1,0:T(8,128)(2,1)S(1)} %copy-done.3, ...), custom_call_target="tpu_custom_call" | custom-call | flops 5000000000 | bytes 15000000 | tf_op jit(solution)/shard_map/stack/pallas_call | solution.py:205
  26.2 0.5 collective-permute-done.7.refs_0_
  26.7 2.3 %stack.6 = (f32[4,96,128]{2,1,0:T(8,128)S(1)}, f32[4,96,128]{2,1,0:T(8,128)S(1)}, bf16[8,4,192,128]{3,2,1,0:T(8,128)(2,1)S(1)}) custom-call(s32[32]{0:T(128)S(1)} %get-tuple-element.26.time_ref, s32[32]{0:T(128)S(1)} %pad_add_fusion.2.rate_ref, bf16[96,512]{1,0:T(8,128)(2,1)S(1)} %copy-done.3, bf16[176,768]{1,0:T(8,128)(2,1)S(1)} %collective-permute-done.7.refs_0_, ...), custom_call_target="tpu_custom_call" | custom-call | flops 5000000000 | bytes 15000000 | tf_op jit(solution)/shard_map/stack/pallas_call | solution.py:205
  29.0 0.1 collective-permute-start.8
  29.1 1.3 %collective-permute-done.8 = f16[4,96,128]{2,1,0:T(8,128)(2,1)S(1)} collective-permute-done((f16[4,96,128]{2,1,0:T(8,128)(2,1)S(1)}, f16[4,96,128]{2,1,0:T(8,128)(2,1)S(1)}, u32[]{:S(2)}, u32[]{:S(2)}) %collective-permute-start.8) | collective-permute-done | bytes 98336 | tf_op jit(solution)/shard_map/ppermute | solution.py:166
  30.4 1.8 %collective-permute-start.9 = (f16[4,96,128]{2,1,0:T(8,128)(2,1)S(1)}, f16[4,96,128]{2,1,0:T(8,128)(2,1)S(1)}, u32[]{:S(2)}, u32[]{:S(2)}) collective-permute-start(f16[4,96,128]{2,1,0:T(8,128)(2,1)S(1)} %add_convert_fusion), channel_id=1, source_target_pairs={{0,8},{1,9},{2,10},{3,11},{4,12},{5,13},{6,14},{7,15},{8,0},{9,1},... | collective-permute-start | bytes 294920 | tf_op jit(solution)/shard_map/ppermute | solution.py:166
  32.3 3.5 %stack.7 = (f32[4,96,128]{2,1,0:T(8,128)S(1)}, f32[4,96,128]{2,1,0:T(8,128)S(1)}) custom-call(s32[32]{0:T(128)S(1)} %get-tuple-element.26.time_ref, s32[32]{0:T(128)S(1)} %pad_add_fusion.2.rate_ref, bf16[96,512]{1,0:T(8,128)(2,1)S(1)} %copy-done.3, bf16[8,4,192,128]{3,2,1,0:T(8,128)(2,1)S(1)} %get-tuple-element.35.refs_0_, ...), custom_call_target="tpu_custom_call" | custom-call | flops 5000000000 | bytes 15000000 | tf_op jit(solution)/shard_map/stack/pallas_call | solution.py:205
  35.8 2.6 %collective-permute-done.9 = f16[4,96,128]{2,1,0:T(8,128)(2,1)S(1)} collective-permute-done((f16[4,96,128]{2,1,0:T(8,128)(2,1)S(1)}, f16[4,96,128]{2,1,0:T(8,128)(2,1)S(1)}, u32[]{:S(2)}, u32[]{:S(2)}) %collective-permute-start.9) | collective-permute-done | bytes 98336 | tf_op jit(solution)/shard_map/ppermute | solution.py:166
  38.4 0.1 collective-permute-start.10
  38.5 1.3 %collective-permute-done.10 = f16[4,96,128]{2,1,0:T(8,128)(2,1)S(1)} collective-permute-done((f16[4,96,128]{2,1,0:T(8,128)(2,1)S(1)}, f16[4,96,128]{2,1,0:T(8,128)(2,1)S(1)}, u32[]{:S(2)}, u32[]{:S(2)}) %collective-permute-start.10) | collective-permute-done | bytes 98336 | tf_op jit(solution)/shard_map/ppermute | solution.py:166
  39.8 0.1 fusion
  39.8 0.2 collective-permute-start.11
  40.1 0.0 collective-permute-start.12
  40.1 2.6 %collective-permute-start.13 = (f16[96,128]{1,0:T(8,128)(2,1)S(1)}, f16[96,128]{1,0:T(8,128)(2,1)S(1)}, u32[]{:S(2)}, u32[]{:S(2)}) collective-permute-start(f16[96,128]{1,0:T(8,128)(2,1)S(1)} %get-tuple-element.50), channel_id=1, source_target_pairs={{0,9},{1,8},{2,11},{3,10},{4,13},{5,12},{6,15},{7,14},{8,1},{9,0},... | collective-permute-start | bytes 73736 | tf_op jit(solution)/shard_map/ppermute | solution.py:166
  42.7 0.0 collective-permute-done.11
  42.7 2.4 %collective-permute-done.12 = f16[96,128]{1,0:T(8,128)(2,1)S(1)} collective-permute-done((f16[96,128]{1,0:T(8,128)(2,1)S(1)}, f16[96,128]{1,0:T(8,128)(2,1)S(1)}, u32[]{:S(2)}, u32[]{:S(2)}) %collective-permute-start.12) | collective-permute-done | bytes 24608 | tf_op jit(solution)/shard_map/ppermute | solution.py:166
  45.1 0.3 collective-permute-done.13
  45.4 2.2 %collective-permute-start.14 = (f16[192,128]{1,0:T(8,128)(2,1)S(1)}, f16[192,128]{1,0:T(8,128)(2,1)S(1)}, u32[]{:S(2)}, u32[]{:S(2)}) collective-permute-start(f16[192,128]{1,0:T(8,128)(2,1)S(1)} %get-tuple-element.68), channel_id=1, source_target_pairs={{0,6},{1,7},{2,4},{3,5},{4,2},{5,3},{6,0},{7,1},{8,14},{9,15},{10,... | collective-permute-start | bytes 147464 | tf_op jit(solution)/shard_map/ppermute | solution.py:166
  47.7 0.3 collective-permute-start.15
  47.9 1.1 %collective-permute-start.16 = (f16[192,128]{1,0:T(8,128)(2,1)S(1)}, f16[192,128]{1,0:T(8,128)(2,1)S(1)}, u32[]{:S(2)}, u32[]{:S(2)}) collective-permute-start(f16[192,128]{1,0:T(8,128)(2,1)S(1)} %get-tuple-element.66), channel_id=1, source_target_pairs={{0,2},{1,3},{2,0},{3,1},{4,6},{5,7},{6,4},{7,5},{8,10},{9,11},{10,... | collective-permute-start | bytes 147464 | tf_op jit(solution)/shard_map/ppermute | solution.py:166
  49.1 1.5 %collective-permute-done.14 = f16[192,128]{1,0:T(8,128)(2,1)S(1)} collective-permute-done((f16[192,128]{1,0:T(8,128)(2,1)S(1)}, f16[192,128]{1,0:T(8,128)(2,1)S(1)}, u32[]{:S(2)}, u32[]{:S(2)}) %collective-permute-start.14) | collective-permute-done | bytes 49184 | tf_op jit(solution)/shard_map/ppermute | solution.py:166
  50.5 1.2 %collective-permute-done.15 = f16[192,128]{1,0:T(8,128)(2,1)S(1)} collective-permute-done((f16[192,128]{1,0:T(8,128)(2,1)S(1)}, f16[192,128]{1,0:T(8,128)(2,1)S(1)}, u32[]{:S(2)}, u32[]{:S(2)}) %collective-permute-start.15) | collective-permute-done | bytes 49184 | tf_op jit(solution)/shard_map/ppermute | solution.py:166
  51.8 0.3 collective-permute-done.16
  52.0 0.1 broadcast_select_fusion.7
  52.1 0.1 convert_multiply_fusion
  52.2 0.8 %fusion.1 = (f32[96,512]{1,0:T(8,128)}, f32[1,96,512]{2,1,0:T(8,128)}) fusion(f32[192,512]{1,0:T(8,128)S(1)} %convert_multiply_fusion), kind=kLoop, calls=%fused_computation.26 | loop fusion | bytes 786432 | tf_op jit(solution)/shard_map/slice | solution.py:252
  (7 shorter events, 0.2 us)
Async XLA Ops:
  0.6 10.8 %collective-permute-start = (s32[2]{0:T(128)}, s32[2]{0:T(128)S(1)}, u32[]{:S(2)}, u32[]{:S(2)}) collective-permute-start(s32[2]{0:T(128)} %bitcast.14), channel_id=1, source_target_pairs={{0,2},{1,3},{2,0},{3,1},{4,6},{5,7},{6,4},{7,5},{8,10},{9,11},{10,... | collective-permute-start | bytes 32 | tf_op jit(solution)/shard_map/ppermute | solution.py:166
  3.7 7.8 %collective-permute-start.1 = (s32[2]{0:T(128)}, s32[2]{0:T(128)S(1)}, u32[]{:S(2)}, u32[]{:S(2)}) collective-permute-start(s32[2]{0:T(128)} %bitcast.15), channel_id=1, source_target_pairs={{0,4},{1,5},{2,6},{3,7},{4,0},{5,1},{6,2},{7,3},{8,12},{9,13},{10,... | collective-permute-start | bytes 32 | tf_op jit(solution)/shard_map/ppermute | solution.py:166
  5.2 6.2 %collective-permute-start.2 = (s32[2]{0:T(128)}, s32[2]{0:T(128)S(1)}, u32[]{:S(2)}, u32[]{:S(2)}) collective-permute-start(s32[2]{0:T(128)} %bitcast.16), channel_id=1, source_target_pairs={{0,6},{1,7},{2,4},{3,5},{4,2},{5,3},{6,0},{7,1},{8,14},{9,15},{10,... | collective-permute-start | bytes 32 | tf_op jit(solution)/shard_map/ppermute | solution.py:166
  5.2 1.1 %copy-start = (bf16[8,96,512]{2,1,0:T(8,128)(2,1)S(1)}, bf16[8,96,512]{2,1,0:T(8,128)(2,1)}, u32[]{:S(2)}) copy-start(bf16[8,96,512]{2,1,0:T(8,128)(2,1)} %param.5) | copy-start | bytes 2359300
  6.4 0.7 %copy-start.1 = (s32[64]{0:T(128)S(1)}, s32[64]{0:T(128)}, u32[]{:S(2)}) copy-start(s32[64]{0:T(128)} %slot_ref.1) | copy-start | bytes 772
  7.0 0.7 %copy-start.2 = (s32[64]{0:T(128)S(1)}, s32[64]{0:T(128)}, u32[]{:S(2)}) copy-start(s32[64]{0:T(128)} %epoch_time_ref.1) | copy-start | bytes 772
  7.7 3.8 %copy-start.4 = (s32[1,2]{1,0:T(1,128)S(1)}, s32[1,2]{1,0:T(1,128)}, u32[]{:S(2)}) copy-start(s32[1,2]{1,0:T(1,128)} %param.6) | copy-start | bytes 28
  7.7 10.2 %copy-start.3 = (bf16[96,512]{1,0:T(8,128)(2,1)S(1)}, bf16[96,512]{1,0:T(8,128)(2,1)}, u32[]{:S(2)}) copy-start(bf16[96,512]{1,0:T(8,128)(2,1)} %constant.44.clone.filter_ref) | copy-start | bytes 294916
  9.5 12.3 %collective-permute-start.5 = (bf16[176,768]{1,0:T(8,128)(2,1)S(1)}, bf16[176,768]{1,0:T(8,128)(2,1)S(1)}, u32[]{:S(2)}, u32[]{:S(2)}) collective-permute-start(bf16[176,768]{1,0:T(8,128)(2,1)S(1)} %get-tuple-element.30), channel_id=1, source_target_pairs={{0,2},{1,3},{2,0},{3,1},{4,6},{5,7},{6,4},{7,5},{8,10},{9,11},{10,... | collective-permute-start | bytes 811016 | tf_op jit(solution)/shard_map/ppermute | solution.py:166
  11.6 4.4 %collective-permute-start.3 = (s32[8]{0:T(128)S(1)}, s32[8]{0:T(128)S(1)}, u32[]{:S(2)}, u32[]{:S(2)}) collective-permute-start(s32[8]{0:T(128)S(1)} %pad_add_fusion), channel_id=1, source_target_pairs={{0,8},{1,9},{2,10},{3,11},{4,12},{5,13},{6,14},{7,15},{8,0},{9,1},... | collective-permute-start | bytes 104 | tf_op jit(solution)/shard_map/ppermute | solution.py:166
  14.2 8.7 %collective-permute-start.6 = (bf16[176,768]{1,0:T(8,128)(2,1)S(1)}, bf16[176,768]{1,0:T(8,128)(2,1)S(1)}, u32[]{:S(2)}, u32[]{:S(2)}) collective-permute-start(bf16[176,768]{1,0:T(8,128)(2,1)S(1)} %get-tuple-element.31), channel_id=1, source_target_pairs={{0,4},{1,5},{2,6},{3,7},{4,0},{5,1},{6,2},{7,3},{8,12},{9,13},{10,... | collective-permute-start | bytes 811016 | tf_op jit(solution)/shard_map/ppermute | solution.py:166
  16.1 1.7 %collective-permute-start.4 = (s32[16]{0:T(128)S(1)}, s32[16]{0:T(128)S(1)}, u32[]{:S(2)}, u32[]{:S(2)}) collective-permute-start(s32[16]{0:T(128)S(1)} %pad_add_fusion.1), channel_id=1, source_target_pairs={{0,1},{1,0},{2,3},{3,2},{4,5},{5,4},{6,7},{7,6},{8,9},{9,8},{10,11... | collective-permute-start | bytes 200 | tf_op jit(solution)/shard_map/ppermute | solution.py:166
  16.1 10.6 %collective-permute-start.7 = (bf16[176,768]{1,0:T(8,128)(2,1)S(1)}, bf16[176,768]{1,0:T(8,128)(2,1)S(1)}, u32[]{:S(2)}, u32[]{:S(2)}) collective-permute-start(bf16[176,768]{1,0:T(8,128)(2,1)S(1)} %get-tuple-element.37), channel_id=1, source_target_pairs={{0,6},{1,7},{2,4},{3,5},{4,2},{5,3},{6,0},{7,1},{8,14},{9,15},{10,... | collective-permute-start | bytes 811016 | tf_op jit(solution)/shard_map/ppermute | solution.py:166
  29.0 1.4 %collective-permute-start.8 = (f16[4,96,128]{2,1,0:T(8,128)(2,1)S(1)}, f16[4,96,128]{2,1,0:T(8,128)(2,1)S(1)}, u32[]{:S(2)}, u32[]{:S(2)}) collective-permute-start(f16[4,96,128]{2,1,0:T(8,128)(2,1)S(1)} %convert_element_type.24), channel_id=1, source_target_pairs={{0,1},{1,0},{2,3},{3,2},{4,5},{5,4},{6,7},{7,6},{8,9},{9,8},{10,11... | collective-permute-start | bytes 294920 | tf_op jit(solution)/shard_map/ppermute | solution.py:166
  30.4 7.9 %collective-permute-start.9 = (f16[4,96,128]{2,1,0:T(8,128)(2,1)S(1)}, f16[4,96,128]{2,1,0:T(8,128)(2,1)S(1)}, u32[]{:S(2)}, u32[]{:S(2)}) collective-permute-start(f16[4,96,128]{2,1,0:T(8,128)(2,1)S(1)} %add_convert_fusion), channel_id=1, source_target_pairs={{0,8},{1,9},{2,10},{3,11},{4,12},{5,13},{6,14},{7,15},{8,0},{9,1},... | collective-permute-start | bytes 294920 | tf_op jit(solution)/shard_map/ppermute | solution.py:166
  38.4 1.4 %collective-permute-start.10 = (f16[4,96,128]{2,1,0:T(8,128)(2,1)S(1)}, f16[4,96,128]{2,1,0:T(8,128)(2,1)S(1)}, u32[]{:S(2)}, u32[]{:S(2)}) collective-permute-start(f16[4,96,128]{2,1,0:T(8,128)(2,1)S(1)} %convert_element_type.27), channel_id=1, source_target_pairs={{0,1},{1,0},{2,3},{3,2},{4,5},{5,4},{6,7},{7,6},{8,9},{9,8},{10,11... | collective-permute-start | bytes 294920 | tf_op jit(solution)/shard_map/ppermute | solution.py:166
  39.8 2.9 %collective-permute-start.11 = (f16[96,128]{1,0:T(8,128)(2,1)S(1)}, f16[96,128]{1,0:T(8,128)(2,1)S(1)}, u32[]{:S(2)}, u32[]{:S(2)}) collective-permute-start(f16[96,128]{1,0:T(8,128)(2,1)S(1)} %get-tuple-element.50), channel_id=1, source_target_pairs={{0,1},{1,0},{2,3},{3,2},{4,5},{5,4},{6,7},{7,6},{8,9},{9,8},{10,11... | collective-permute-start | bytes 73736 | tf_op jit(solution)/shard_map/ppermute | solution.py:166
  40.1 5.0 %collective-permute-start.12 = (f16[96,128]{1,0:T(8,128)(2,1)S(1)}, f16[96,128]{1,0:T(8,128)(2,1)S(1)}, u32[]{:S(2)}, u32[]{:S(2)}) collective-permute-start(f16[96,128]{1,0:T(8,128)(2,1)S(1)} %get-tuple-element.50), channel_id=1, source_target_pairs={{0,8},{1,9},{2,10},{3,11},{4,12},{5,13},{6,14},{7,15},{8,0},{9,1},... | collective-permute-start | bytes 73736 | tf_op jit(solution)/shard_map/ppermute | solution.py:166
  40.1 5.3 %collective-permute-start.13 = (f16[96,128]{1,0:T(8,128)(2,1)S(1)}, f16[96,128]{1,0:T(8,128)(2,1)S(1)}, u32[]{:S(2)}, u32[]{:S(2)}) collective-permute-start(f16[96,128]{1,0:T(8,128)(2,1)S(1)} %get-tuple-element.50), channel_id=1, source_target_pairs={{0,9},{1,8},{2,11},{3,10},{4,13},{5,12},{6,15},{7,14},{8,1},{9,0},... | collective-permute-start | bytes 73736 | tf_op jit(solution)/shard_map/ppermute | solution.py:166
  45.4 5.1 %collective-permute-start.14 = (f16[192,128]{1,0:T(8,128)(2,1)S(1)}, f16[192,128]{1,0:T(8,128)(2,1)S(1)}, u32[]{:S(2)}, u32[]{:S(2)}) collective-permute-start(f16[192,128]{1,0:T(8,128)(2,1)S(1)} %get-tuple-element.68), channel_id=1, source_target_pairs={{0,6},{1,7},{2,4},{3,5},{4,2},{5,3},{6,0},{7,1},{8,14},{9,15},{10,... | collective-permute-start | bytes 147464 | tf_op jit(solution)/shard_map/ppermute | solution.py:166
  47.7 4.1 %collective-permute-start.15 = (f16[192,128]{1,0:T(8,128)(2,1)S(1)}, f16[192,128]{1,0:T(8,128)(2,1)S(1)}, u32[]{:S(2)}, u32[]{:S(2)}) collective-permute-start(f16[192,128]{1,0:T(8,128)(2,1)S(1)} %get-tuple-element.67), channel_id=1, source_target_pairs={{0,4},{1,5},{2,6},{3,7},{4,0},{5,1},{6,2},{7,3},{8,12},{9,13},{10,... | collective-permute-start | bytes 147464 | tf_op jit(solution)/shard_map/ppermute | solution.py:166
  47.9 4.1 %collective-permute-start.16 = (f16[192,128]{1,0:T(8,128)(2,1)S(1)}, f16[192,128]{1,0:T(8,128)(2,1)S(1)}, u32[]{:S(2)}, u32[]{:S(2)}) collective-permute-start(f16[192,128]{1,0:T(8,128)(2,1)S(1)} %get-tuple-element.66), channel_id=1, source_target_pairs={{0,2},{1,3},{2,0},{3,1},{4,6},{5,7},{6,4},{7,5},{8,10},{9,11},{10,... | collective-permute-start | bytes 147464 | tf_op jit(solution)/shard_map/ppermute | solution.py:166

commit v4 on v3

--- a/solution.py
+++ b/solution.py
@@ -19,7 +19,6 @@
     np.float32,
 )
 spline_norm = 147456.0
-rate_divisor = 32
 HALO = 24
 LANES = 128
 PACK = 16
@@ -35,16 +34,9 @@
     return band.astype(ml_dtypes.bfloat16)
 
 
-def window_kernel(block, per_device, device_ref, slot_ref, epoch_time_ref, image_ref, time_ref, *refs):
+def window_kernel(block, image_ref, *refs):
     *window_refs, padded = refs
-    chips = len(window_refs)
-    epochs = slot_ref.shape[0]
-    place = (device_ref[0] >> 1) & (chips - 1)
-    for relative in range(chips):
-        source = device_ref[0] ^ (2 * relative)
-        for number in range(per_device):
-            slot = lax.rem(source * per_device + number, epochs)
-            time_ref[relative * per_device + number] = epoch_time_ref[slot_ref[slot]]
+    place = (lax.axis_index("vel") >> 1) & (len(window_refs) - 1)
     lanes, columns = image_ref.shape
     image = jnp.concatenate([image_ref[...], jnp.zeros((lanes, LANES), image_ref.dtype)], axis=1)
     image = pltpu.roll(image, HALO, 1)
@@ -55,21 +47,23 @@
         window_ref[...] = padded[pl.ds(start, block + 2 * HALO)]
 
 
-def stack_kernel(block, rows, sources, images, first, scale, fresh, carried, time_ref, rate_ref, filter_ref, *refs):
+def stack_kernel(block, rows, sources, images, first, scale, fresh, carried, slot_ref, time_ref, rate_ref, filter_ref, *refs):
     count = len(sources)
     given, before, refs = refs[:count], refs[count:][:carried], refs[count + carried :]
     keep_ref, send_ref, *refs = refs
     kept, refs = (refs[:count], refs[count:]) if fresh else (given, refs)
-    bands, own, times, rates, semaphores, *bins = refs
+    bands, own, slots, times, rates, semaphores, *bins = refs
     fetches = [
-        pltpu.make_async_copy(time_ref, times, semaphores.at[0]),
-        pltpu.make_async_copy(rate_ref, rates, semaphores.at[1]),
+        pltpu.make_async_copy(slot_ref, slots, semaphores.at[0]),
+        pltpu.make_async_copy(time_ref, times, semaphores.at[1]),
+        pltpu.make_async_copy(rate_ref, rates, semaphores.at[2]),
     ]
     for fetch in fetches:
         fetch.start()
     if fresh and sources[0] == 0:
-        copy = pltpu.make_async_copy(given[0], own, semaphores.at[2])
+        copy = pltpu.make_async_copy(given[0], own, semaphores.at[3])
         copy.start()
+    chips = rates.shape[0] // 8
     together = len(bins)
     turns = bins[0].shape[0] // 4
     reach = bins[0].shape[1] - PACK
@@ -102,12 +96,13 @@
             if index == 0 and number == 0:
                 for fetch in fetches:
                     fetch.wait()
-            time = times[relative * images + number]
+            source = lax.axis_index("vel") ^ (2 * relative)
+            time = times[slots[lax.rem(source * images + number, times.shape[0])]]
 
             def add(turn, _, time=time, number=number, filtered=filtered):
                 for lane in range(together):
                     v = first + turn * together + lane
-                    rate = (v & 1) * (rates.shape[0] // 2) + (v >> 1) * 2
+                    rate = (v >> 1) // chips * 4 * chips + (v & 1) * 2 * chips + (v >> 1) % chips * 2
                     row_offset = (rates[rate] * time) >> 5
                     column_offset = (rates[rate + 1] * time) >> 5
                     start = HALO - 1 + (column_offset >> 2)
@@ -155,7 +150,6 @@
 
 def local(axis_size, epoch_maps, velocity, slot_epoch, epoch_time):
     per_device, rows, columns = epoch_maps.shape
-    epochs = slot_epoch.shape[0]
     half = axis_size // 2
     chips = half // 2
     block = columns // chips
@@ -178,20 +172,20 @@
 
     rates = velocity.reshape(-1)
     rates = jnp.concatenate([rates] + [swap(rates, 2 * x) for x in range(1, chips)])
-    times, *windows = pl.pallas_call(
-        functools.partial(window_kernel, block, per_device),
-        out_shape=[shape((chips * per_device,), jnp.int32)] + [shape((wide, lanes), epoch_maps.dtype)] * chips,
-        in_specs=[smem] * 3 + [vmem],
-        out_specs=[smem] + [vmem] * chips,
+    windows = list(pl.pallas_call(
+        functools.partial(window_kernel, block),
+        out_shape=[shape((wide, lanes), epoch_maps.dtype)] * chips,
+        in_specs=[vmem],
+        out_specs=[vmem] * chips,
         scratch_shapes=[pltpu.VMEM((columns + LANES, lanes), epoch_maps.dtype)],
-        compiler_params=pltpu.CompilerParams(vmem_limit_bytes=16 * 1024 * 1024),
+        compiler_params=pltpu.CompilerParams(vmem_limit_bytes=56 * 1024 * 1024),
         cost_estimate=cost(3),
         name="windows",
-    )(device.reshape(1), slot_epoch, epoch_time, epoch_maps.reshape(lanes, columns))
-
+    )(epoch_maps.reshape(lanes, columns)))
+    late = [chips - 1]
     windows[2:], rates = lax.optimization_barrier((windows[2:], rates))
+    rates = jnp.concatenate([rates, swap(rates, 1)])
     rates = jnp.concatenate([rates, swap(rates, half)])
-    rates = jnp.concatenate([rates, swap(rates, 1)])
     windows = [windows[0]] + [swap(windows[x], 2 * x) for x in range(1, chips)]
 
     reach = (block + 2 + PACK + PACK - 1) // PACK * PACK
@@ -208,36 +202,33 @@
                 *(block, rows, sources, per_device, first, LINK_SCALE / spline_norm, fresh, len(carried)),
             ),
             out_shape=[shape((count // 2, rows, block), jnp.float32)] * 2 + [filtered] * (fresh * len(sources)),
-            in_specs=[hbm, hbm, vmem]
+            in_specs=[hbm, hbm, hbm, vmem]
             + [hbm if x == 0 and fresh else vmem for x in sources]
             + [vmem] * len(carried),
             out_specs=[vmem] * (2 + fresh * len(sources)),
             scratch_shapes=[
                 pltpu.VMEM((4, 2 * LANES, 4 * LANES), jnp.bfloat16),
                 pltpu.VMEM((wide, lanes), jnp.bfloat16),
-                pltpu.SMEM(times.shape, jnp.int32),
+                pltpu.SMEM(slot_epoch.shape, jnp.int32),
+                pltpu.SMEM(epoch_time.shape, jnp.int32),
                 pltpu.SMEM(rates.shape, jnp.int32),
-                pltpu.SemaphoreType.DMA((3,)),
+                pltpu.SemaphoreType.DMA((4,)),
             ]
             + [pltpu.VMEM((4 * count // together, reach + PACK, LANES), jnp.float32)] * together,
             compiler_params=pltpu.CompilerParams(vmem_limit_bytes=32 * 1024 * 1024),
             cost_estimate=cost(5),
             name="stack",
-        )(times, rates, band, *given, *carried)
+        )(slot_epoch, epoch_time, rates, band, *given, *carried)
         return keep, send, filtered
 
-    late = [chips - 1]
-    early = [x for x in range(1, chips) if x not in late]
-    keep, send, _ = stack([0], 0, axis_size, windows[:1])
-    far, early_rows = (keep[chips:], send[chips:]), []
-    if early:
-        *far, early_rows = stack(early, half, half, [windows[x] for x in early], far)
+    early = list(range(chips - 1))
+    *far, early_rows = stack(early, half, half, [windows[x] for x in early])
     keep_far, send_far, late_rows = stack(late, half, half, [windows[x] for x in late], far)
     far = keep_far + swap(send_far.astype(jnp.float16), 1).astype(jnp.float32)
     far = far.astype(jnp.float16)
-    far, near = lax.optimization_barrier((far, (keep[:chips], send[:chips])))
+    far, early_rows = lax.optimization_barrier((far, early_rows))
     other = swap(far, half).astype(jnp.float32) * (1.0 / LINK_SCALE)
-    keep_near, send_near, _ = stack(early + late, 0, half, early_rows + late_rows, near, fresh=False)
+    keep_near, send_near, _ = stack(early + late, 0, half, early_rows + late_rows, fresh=False)
     send_near, other = lax.optimization_barrier((send_near.astype(jnp.float16), other))
     near = (keep_near + swap(send_near, 1).astype(jnp.float32)) * (1.0 / LINK_SCALE)
     first = device < half

time: 53.1 us -> 51.3 us (0.966)
  local copies, waits for them, and re-layouts: 3.29 us -> 1.75 us
  waiting for transfers between devices: 12.6 us -> 13.9 us
  Pallas kernels: 14.8 us -> 13.8 us
    pallas_call x4 -> x3, Pallas kernels: 13 us -> 11 us  [stack(): pl.pallas_call(functools.partial(stack_kernel, *(block, rows, sources, pe...]
    unnamed x10, local copies, waits for them, and re-layouts: 2.45 us -> 0.96 us
    ppermute x17, waiting for transfers between devices: 12.6 us -> 13.9 us  [swap(): return lax.ppermute(array, 'vel', [(i, i ^ bits) for i in range(axis_size)])]
    pallas_call x1, Pallas kernels: 1.8 us -> 2.78 us  [local(): pl.pallas_call(functools.partial(window_kernel, block), out_shape=[shape(...]
  transfers between devices with their start and end apart: 17 -> 17, of which waited for: 11 -> 10; matrix products, arithmetic and copies ran while one was open for 1% -> 1% of each run, Pallas kernels for 24% -> 22%
where the time goes in v4:
time: 51.3 us; the launch traced here: 51.2 us
  starting transfers between devices  20.3 us (40%)
  waiting for transfers between devices  13.9 us (27%)
  Pallas kernels  13.8 us (27%)
  local copies, waits for them, and re-layouts  1.75 us (3%)
  between operations  0.79 us (2%)
  other arithmetic  0.58 us (1%)
    ppermute x17, starting transfers between devices, swap(): return lax.ppermute(array, 'vel', [(i, i ^ bits) for i in range(axis_size)])  20.3 us
    ppermute x17, waiting for transfers between devices, swap(): return lax.ppermute(array, 'vel', [(i, i ^ bits) for i in range(axis_size)])  13.9 us
    pallas_call x3, Pallas kernels, stack(): pl.pallas_call(functools.partial(stack_kernel, *(block, rows, sources, pe...  11 us
    pallas_call x1, Pallas kernels, local(): pl.pallas_call(functools.partial(window_kernel, block), out_shape=[shape(...  2.78 us
  transfers between devices with their start and end apart: 17, of which 10 were waited for; matrix products, arithmetic and copies ran while one was open for 1% of the time, Pallas kernels for 22%

profile of v4, /device:TPU:0, one launch (start us, length us, event | category | flops | bytes accessed | tf_op | source)
XLA Modules:
  0.0 51.2 jit_solution(11860164588534980245)
XLA Ops:
  0.6 3.0 %collective-permute-start = (s32[2]{0:T(128)}, s32[2]{0:T(128)S(1)}, u32[]{:S(2)}, u32[]{:S(2)}) collective-permute-start(s32[2]{0:T(128)} %bitcast.12), channel_id=1, source_target_pairs={{0,2},{1,3},{2,0},{3,1},{4,6},{5,7},{6,4},{7,5},{8,10},{9,11},{10,... | collective-permute-start | bytes 32 | tf_op jit(solution)/shard_map/ppermute | solution.py:160
  3.7 1.6 %collective-permute-start.1 = (s32[2]{0:T(128)}, s32[2]{0:T(128)S(1)}, u32[]{:S(2)}, u32[]{:S(2)}) collective-permute-start(s32[2]{0:T(128)} %bitcast.13), channel_id=1, source_target_pairs={{0,4},{1,5},{2,6},{3,7},{4,0},{5,1},{6,2},{7,3},{8,12},{9,13},{10,... | collective-permute-start | bytes 32 | tf_op jit(solution)/shard_map/ppermute | solution.py:160
  5.2 0.0 collective-permute-start.2
  5.2 0.0 copy-start.4
  5.2 0.0 copy-start
  5.2 0.0 copy-start.1
  5.3 0.0 copy-start.2
  5.3 2.8 %windows.1 = (bf16[176,768]{1,0:T(8,128)(2,1)}, bf16[176,768]{1,0:T(8,128)(2,1)}, bf16[176,768]{1,0:T(8,128)(2,1)}, bf16[176,768]{1,0:T(8,128)(2,1)}) custom-call(bf16[768,512]{1,0:T(8,128)(2,1)} %bitcast.16), custom_call_target="tpu_custom_call" | custom-call | flops 3000000000 | bytes 9000000 | tf_op jit(solution)/shard_map/windows/pallas_call | solution.py:175
  8.0 1.9 %collective-permute-start.6 = (bf16[176,768]{1,0:T(8,128)(2,1)}, bf16[176,768]{1,0:T(8,128)(2,1)S(1)}, u32[]{:S(2)}, u32[]{:S(2)}) collective-permute-start(bf16[176,768]{1,0:T(8,128)(2,1)} %get-tuple-element.30), channel_id=1, source_target_pairs={{0,2},{1,3},{2,0},{3,1},{4,6},{5,7},{6,4},{7,5},{8,10},{9,11},{10,... | collective-permute-start | bytes 811016 | tf_op jit(solution)/shard_map/ppermute | solution.py:160
  9.9 0.0 collective-permute-done
  9.9 0.0 collective-permute-done.1
  10.0 0.0 collective-permute-done.2
  10.0 0.0 copy-done.4
  10.0 0.1 pad_add_fusion
  10.0 1.6 %collective-permute-start.7 = (bf16[176,768]{1,0:T(8,128)(2,1)}, bf16[176,768]{1,0:T(8,128)(2,1)S(1)}, u32[]{:S(2)}, u32[]{:S(2)}) collective-permute-start(bf16[176,768]{1,0:T(8,128)(2,1)} %get-tuple-element.31), channel_id=1, source_target_pairs={{0,4},{1,5},{2,6},{3,7},{4,0},{5,1},{6,2},{7,3},{8,12},{9,13},{10,... | collective-permute-start | bytes 811016 | tf_op jit(solution)/shard_map/ppermute | solution.py:160
  11.6 0.0 collective-permute-start.3
  11.6 1.1 %collective-permute-done.3 = s32[8]{0:T(128)S(1)} collective-permute-done((s32[8]{0:T(128)S(1)}, s32[8]{0:T(128)S(1)}, u32[]{:S(2)}, u32[]{:S(2)}) %collective-permute-start.3) | collective-permute-done | bytes 64 | tf_op jit(solution)/shard_map/ppermute | solution.py:160
  12.8 0.1 pad_add_fusion.1
  12.8 2.6 %collective-permute-start.4 = (s32[16]{0:T(128)S(1)}, s32[16]{0:T(128)S(1)}, u32[]{:S(2)}, u32[]{:S(2)}) collective-permute-start(s32[16]{0:T(128)S(1)} %pad_add_fusion.1), channel_id=1, source_target_pairs={{0,8},{1,9},{2,10},{3,11},{4,12},{5,13},{6,14},{7,15},{8,0},{9,1},... | collective-permute-start | bytes 200 | tf_op jit(solution)/shard_map/ppermute | solution.py:160
  15.4 0.4 collective-permute-start.5
  15.8 1.5 %collective-permute-done.4 = s32[16]{0:T(128)S(1)} collective-permute-done((s32[16]{0:T(128)S(1)}, s32[16]{0:T(128)S(1)}, u32[]{:S(2)}, u32[]{:S(2)}) %collective-permute-start.4) | collective-permute-done | bytes 96 | tf_op jit(solution)/shard_map/ppermute | solution.py:160
  17.3 0.1 pad_add_fusion.2.rate_ref
  17.4 0.0 collective-permute-done.6.refs_1_
  17.4 0.0 collective-permute-done.7.refs_2_
  17.4 0.0 copy-done
  17.4 0.0 copy-done.1
  17.4 0.0 copy-done.2
  17.4 0.0 copy-start.3
  17.4 0.9 %copy-done.3 = bf16[176,768]{1,0:T(8,128)(2,1)S(1)} copy-done((bf16[176,768]{1,0:T(8,128)(2,1)S(1)}, bf16[176,768]{1,0:T(8,128)(2,1)}, u32[]{:S(2)}) %copy-start.3) | copy-done | bytes 270360
  18.3 4.5 %stack.3 = (f32[4,96,128]{2,1,0:T(8,128)S(1)}, f32[4,96,128]{2,1,0:T(8,128)S(1)}, bf16[8,4,192,128]{3,2,1,0:T(8,128)(2,1)S(1)}, bf16[8,4,192,128]{3,2,1,0:T(8,128)(2,1)S(1)}, bf16[8,4,192,128]{3,2,1,0:T(8,128)(2,1)S(1)}) custom-call(s32[64]{0:T(128)S(1)} %copy-done, s32[64]{0:T(128)S(1)} %copy-done.1, s32[32]{0:T(128)S(1)} %pad_add_fusion.2.rate_ref, ...), custom_call_target="tpu_custom_call" | custom-call | flops 5000000000 | bytes 15000000 | tf_op jit(solution)/shard_map/stack/pallas_call | solution.py:199
  22.9 2.0 %collective-permute-done.5.refs_0_ = bf16[176,768]{1,0:T(8,128)(2,1)S(1)} collective-permute-done((bf16[176,768]{1,0:T(8,128)(2,1)}, bf16[176,768]{1,0:T(8,128)(2,1)S(1)}, u32[]{:S(2)}, u32[]{:S(2)}) %collective-permute-start.5) | collective-permute-done | bytes 270368 | tf_op jit(solution)/shard_map/ppermute | solution.py:160
  24.9 2.3 %stack.4 = (f32[4,96,128]{2,1,0:T(8,128)S(1)}, f32[4,96,128]{2,1,0:T(8,128)S(1)}, bf16[8,4,192,128]{3,2,1,0:T(8,128)(2,1)S(1)}) custom-call(s32[64]{0:T(128)S(1)} %copy-done, s32[64]{0:T(128)S(1)} %copy-done.1, s32[32]{0:T(128)S(1)} %pad_add_fusion.2.rate_ref, bf16[96,512]{1,0:T(8,128)(2,1)S(1)} %copy-done.2, ...), custom_call_target="tpu_custom_call" | custom-call | flops 5000000000 | bytes 15000000 | tf_op jit(solution)/shard_map/stack/pallas_call | solution.py:199
  27.2 0.1 collective-permute-start.8
  27.3 1.3 %collective-permute-done.8 = f16[4,96,128]{2,1,0:T(8,128)(2,1)S(1)} collective-permute-done((f16[4,96,128]{2,1,0:T(8,128)(2,1)S(1)}, f16[4,96,128]{2,1,0:T(8,128)(2,1)S(1)}, u32[]{:S(2)}, u32[]{:S(2)}) %collective-permute-start.8) | collective-permute-done | bytes 98336 | tf_op jit(solution)/shard_map/ppermute | solution.py:160
  28.6 2.2 %collective-permute-start.9 = (f16[4,96,128]{2,1,0:T(8,128)(2,1)S(1)}, f16[4,96,128]{2,1,0:T(8,128)(2,1)S(1)}, u32[]{:S(2)}, u32[]{:S(2)}) collective-permute-start(f16[4,96,128]{2,1,0:T(8,128)(2,1)S(1)} %add_convert_fusion), channel_id=1, source_target_pairs={{0,8},{1,9},{2,10},{3,11},{4,12},{5,13},{6,14},{7,15},{8,0},{9,1},... | collective-permute-start | bytes 294920 | tf_op jit(solution)/shard_map/ppermute | solution.py:160
  30.8 4.2 %stack.5 = (f32[4,96,128]{2,1,0:T(8,128)S(1)}, f32[4,96,128]{2,1,0:T(8,128)S(1)}) custom-call(s32[64]{0:T(128)S(1)} %copy-done, s32[64]{0:T(128)S(1)} %copy-done.1, s32[32]{0:T(128)S(1)} %pad_add_fusion.2.rate_ref, bf16[96,512]{1,0:T(8,128)(2,1)S(1)} %copy-done.2, bf16[8,4,192,128]{3,2,1,0:T(8,128)(2,1)S(1)} %get-tuple-element.39.refs_0_, ...), custom_call_target="tpu_custom_call" | custom-call | flops 5000000000 | bytes 15000000 | tf_op jit(solution)/shard_map/stack/pallas_call | solution.py:199
  35.0 1.5 %collective-permute-done.9 = f16[4,96,128]{2,1,0:T(8,128)(2,1)S(1)} collective-permute-done((f16[4,96,128]{2,1,0:T(8,128)(2,1)S(1)}, f16[4,96,128]{2,1,0:T(8,128)(2,1)S(1)}, u32[]{:S(2)}, u32[]{:S(2)}) %collective-permute-start.9) | collective-permute-done | bytes 98336 | tf_op jit(solution)/shard_map/ppermute | solution.py:160
  36.5 0.1 collective-permute-start.10
  36.6 1.3 %collective-permute-done.10 = f16[4,96,128]{2,1,0:T(8,128)(2,1)S(1)} collective-permute-done((f16[4,96,128]{2,1,0:T(8,128)(2,1)S(1)}, f16[4,96,128]{2,1,0:T(8,128)(2,1)S(1)}, u32[]{:S(2)}, u32[]{:S(2)}) %collective-permute-start.10) | collective-permute-done | bytes 98336 | tf_op jit(solution)/shard_map/ppermute | solution.py:160
  37.9 0.1 fusion
  38.0 0.2 collective-permute-start.11
  38.2 0.1 collective-permute-start.12
  38.3 2.5 %collective-permute-start.13 = (f16[96,128]{1,0:T(8,128)(2,1)S(1)}, f16[96,128]{1,0:T(8,128)(2,1)S(1)}, u32[]{:S(2)}, u32[]{:S(2)}) collective-permute-start(f16[96,128]{1,0:T(8,128)(2,1)S(1)} %get-tuple-element.48), channel_id=1, source_target_pairs={{0,9},{1,8},{2,11},{3,10},{4,13},{5,12},{6,15},{7,14},{8,1},{9,0},... | collective-permute-start | bytes 73736 | tf_op jit(solution)/shard_map/ppermute | solution.py:160
  40.8 0.0 collective-permute-done.11
  40.8 2.5 %collective-permute-done.12 = f16[96,128]{1,0:T(8,128)(2,1)S(1)} collective-permute-done((f16[96,128]{1,0:T(8,128)(2,1)S(1)}, f16[96,128]{1,0:T(8,128)(2,1)S(1)}, u32[]{:S(2)}, u32[]{:S(2)}) %collective-permute-start.12) | collective-permute-done | bytes 24608 | tf_op jit(solution)/shard_map/ppermute | solution.py:160
  43.4 0.0 collective-permute-done.13
  43.4 2.4 %collective-permute-start.14 = (f16[192,128]{1,0:T(8,128)(2,1)S(1)}, f16[192,128]{1,0:T(8,128)(2,1)S(1)}, u32[]{:S(2)}, u32[]{:S(2)}) collective-permute-start(f16[192,128]{1,0:T(8,128)(2,1)S(1)} %get-tuple-element.62), channel_id=1, source_target_pairs={{0,6},{1,7},{2,4},{3,5},{4,2},{5,3},{6,0},{7,1},{8,14},{9,15},{10,... | collective-permute-start | bytes 147464 | tf_op jit(solution)/shard_map/ppermute | solution.py:160
  45.8 0.4 collective-permute-start.15
  46.2 1.4 %collective-permute-start.16 = (f16[192,128]{1,0:T(8,128)(2,1)S(1)}, f16[192,128]{1,0:T(8,128)(2,1)S(1)}, u32[]{:S(2)}, u32[]{:S(2)}) collective-permute-start(f16[192,128]{1,0:T(8,128)(2,1)S(1)} %get-tuple-element.60), channel_id=1, source_target_pairs={{0,2},{1,3},{2,0},{3,1},{4,6},{5,7},{6,4},{7,5},{8,10},{9,11},{10,... | collective-permute-start | bytes 147464 | tf_op jit(solution)/shard_map/ppermute | solution.py:160
  47.5 0.9 %collective-permute-done.14 = f16[192,128]{1,0:T(8,128)(2,1)S(1)} collective-permute-done((f16[192,128]{1,0:T(8,128)(2,1)S(1)}, f16[192,128]{1,0:T(8,128)(2,1)S(1)}, u32[]{:S(2)}, u32[]{:S(2)}) %collective-permute-start.14) | collective-permute-done | bytes 49184 | tf_op jit(solution)/shard_map/ppermute | solution.py:160
  48.5 1.4 %collective-permute-done.15 = f16[192,128]{1,0:T(8,128)(2,1)S(1)} collective-permute-done((f16[192,128]{1,0:T(8,128)(2,1)S(1)}, f16[192,128]{1,0:T(8,128)(2,1)S(1)}, u32[]{:S(2)}, u32[]{:S(2)}) %collective-permute-start.15) | collective-permute-done | bytes 49184 | tf_op jit(solution)/shard_map/ppermute | solution.py:160
  49.9 0.4 collective-permute-done.16
  50.3 0.1 broadcast_select_fusion.7
  50.3 0.1 convert_multiply_fusion
  50.4 0.8 %fusion.1 = (f32[96,512]{1,0:T(8,128)}, f32[1,96,512]{2,1,0:T(8,128)}) fusion(f32[192,512]{1,0:T(8,128)S(1)} %convert_multiply_fusion), kind=kLoop, calls=%fused_computation.26 | loop fusion | bytes 786432 | tf_op jit(solution)/shard_map/slice | solution.py:243
  (7 shorter events, 0.2 us)
Async XLA Ops:
  0.6 9.3 %collective-permute-start = (s32[2]{0:T(128)}, s32[2]{0:T(128)S(1)}, u32[]{:S(2)}, u32[]{:S(2)}) collective-permute-start(s32[2]{0:T(128)} %bitcast.12), channel_id=1, source_target_pairs={{0,2},{1,3},{2,0},{3,1},{4,6},{5,7},{6,4},{7,5},{8,10},{9,11},{10,... | collective-permute-start | bytes 32 | tf_op jit(solution)/shard_map/ppermute | solution.py:160
  3.7 6.3 %collective-permute-start.1 = (s32[2]{0:T(128)}, s32[2]{0:T(128)S(1)}, u32[]{:S(2)}, u32[]{:S(2)}) collective-permute-start(s32[2]{0:T(128)} %bitcast.13), channel_id=1, source_target_pairs={{0,4},{1,5},{2,6},{3,7},{4,0},{5,1},{6,2},{7,3},{8,12},{9,13},{10,... | collective-permute-start | bytes 32 | tf_op jit(solution)/shard_map/ppermute | solution.py:160
  5.2 4.7 %collective-permute-start.2 = (s32[2]{0:T(128)}, s32[2]{0:T(128)S(1)}, u32[]{:S(2)}, u32[]{:S(2)}) collective-permute-start(s32[2]{0:T(128)} %bitcast.14), channel_id=1, source_target_pairs={{0,6},{1,7},{2,4},{3,5},{4,2},{5,3},{6,0},{7,1},{8,14},{9,15},{10,... | collective-permute-start | bytes 32 | tf_op jit(solution)/shard_map/ppermute | solution.py:160
  5.2 4.7 %copy-start.4 = (s32[1,2]{1,0:T(1,128)S(1)}, s32[1,2]{1,0:T(1,128)}, u32[]{:S(2)}) copy-start(s32[1,2]{1,0:T(1,128)} %param.6) | copy-start | bytes 28
  5.2 12.1 %copy-start = (s32[64]{0:T(128)S(1)}, s32[64]{0:T(128)}, u32[]{:S(2)}) copy-start(s32[64]{0:T(128)} %slot_ref.5) | copy-start | bytes 772
  5.2 12.1 %copy-start.1 = (s32[64]{0:T(128)S(1)}, s32[64]{0:T(128)}, u32[]{:S(2)}) copy-start(s32[64]{0:T(128)} %time_ref.5) | copy-start | bytes 772
  5.3 12.1 %copy-start.2 = (bf16[96,512]{1,0:T(8,128)(2,1)S(1)}, bf16[96,512]{1,0:T(8,128)(2,1)}, u32[]{:S(2)}) copy-start(bf16[96,512]{1,0:T(8,128)(2,1)} %constant.44.clone.filter_ref) | copy-start | bytes 294916
  8.0 9.3 %collective-permute-start.6 = (bf16[176,768]{1,0:T(8,128)(2,1)}, bf16[176,768]{1,0:T(8,128)(2,1)S(1)}, u32[]{:S(2)}, u32[]{:S(2)}) collective-permute-start(bf16[176,768]{1,0:T(8,128)(2,1)} %get-tuple-element.30), channel_id=1, source_target_pairs={{0,2},{1,3},{2,0},{3,1},{4,6},{5,7},{6,4},{7,5},{8,10},{9,11},{10,... | collective-permute-start | bytes 811016 | tf_op jit(solution)/shard_map/ppermute | solution.py:160
  10.0 7.3 %collective-permute-start.7 = (bf16[176,768]{1,0:T(8,128)(2,1)}, bf16[176,768]{1,0:T(8,128)(2,1)S(1)}, u32[]{:S(2)}, u32[]{:S(2)}) collective-permute-start(bf16[176,768]{1,0:T(8,128)(2,1)} %get-tuple-element.31), channel_id=1, source_target_pairs={{0,4},{1,5},{2,6},{3,7},{4,0},{5,1},{6,2},{7,3},{8,12},{9,13},{10,... | collective-permute-start | bytes 811016 | tf_op jit(solution)/shard_map/ppermute | solution.py:160
  11.6 1.1 %collective-permute-start.3 = (s32[8]{0:T(128)S(1)}, s32[8]{0:T(128)S(1)}, u32[]{:S(2)}, u32[]{:S(2)}) collective-permute-start(s32[8]{0:T(128)S(1)} %pad_add_fusion), channel_id=1, source_target_pairs={{0,1},{1,0},{2,3},{3,2},{4,5},{5,4},{6,7},{7,6},{8,9},{9,8},{10,11... | collective-permute-start | bytes 104 | tf_op jit(solution)/shard_map/ppermute | solution.py:160
  12.8 4.4 %collective-permute-start.4 = (s32[16]{0:T(128)S(1)}, s32[16]{0:T(128)S(1)}, u32[]{:S(2)}, u32[]{:S(2)}) collective-permute-start(s32[16]{0:T(128)S(1)} %pad_add_fusion.1), channel_id=1, source_target_pairs={{0,8},{1,9},{2,10},{3,11},{4,12},{5,13},{6,14},{7,15},{8,0},{9,1},... | collective-permute-start | bytes 200 | tf_op jit(solution)/shard_map/ppermute | solution.py:160
  15.4 9.4 %collective-permute-start.5 = (bf16[176,768]{1,0:T(8,128)(2,1)}, bf16[176,768]{1,0:T(8,128)(2,1)S(1)}, u32[]{:S(2)}, u32[]{:S(2)}) collective-permute-start(bf16[176,768]{1,0:T(8,128)(2,1)} %get-tuple-element.28), channel_id=1, source_target_pairs={{0,6},{1,7},{2,4},{3,5},{4,2},{5,3},{6,0},{7,1},{8,14},{9,15},{10,... | collective-permute-start | bytes 811016 | tf_op jit(solution)/shard_map/ppermute | solution.py:160
  17.4 1.0 %copy-start.3 = (bf16[176,768]{1,0:T(8,128)(2,1)S(1)}, bf16[176,768]{1,0:T(8,128)(2,1)}, u32[]{:S(2)}) copy-start(bf16[176,768]{1,0:T(8,128)(2,1)} %get-tuple-element.29.refs_0_) | copy-start | bytes 811012
  27.2 1.4 %collective-permute-start.8 = (f16[4,96,128]{2,1,0:T(8,128)(2,1)S(1)}, f16[4,96,128]{2,1,0:T(8,128)(2,1)S(1)}, u32[]{:S(2)}, u32[]{:S(2)}) collective-permute-start(f16[4,96,128]{2,1,0:T(8,128)(2,1)S(1)} %convert_element_type.24), channel_id=1, source_target_pairs={{0,1},{1,0},{2,3},{3,2},{4,5},{5,4},{6,7},{7,6},{8,9},{9,8},{10,11... | collective-permute-start | bytes 294920 | tf_op jit(solution)/shard_map/ppermute | solution.py:160
  28.6 7.9 %collective-permute-start.9 = (f16[4,96,128]{2,1,0:T(8,128)(2,1)S(1)}, f16[4,96,128]{2,1,0:T(8,128)(2,1)S(1)}, u32[]{:S(2)}, u32[]{:S(2)}) collective-permute-start(f16[4,96,128]{2,1,0:T(8,128)(2,1)S(1)} %add_convert_fusion), channel_id=1, source_target_pairs={{0,8},{1,9},{2,10},{3,11},{4,12},{5,13},{6,14},{7,15},{8,0},{9,1},... | collective-permute-start | bytes 294920 | tf_op jit(solution)/shard_map/ppermute | solution.py:160
  36.5 1.4 %collective-permute-start.10 = (f16[4,96,128]{2,1,0:T(8,128)(2,1)S(1)}, f16[4,96,128]{2,1,0:T(8,128)(2,1)S(1)}, u32[]{:S(2)}, u32[]{:S(2)}) collective-permute-start(f16[4,96,128]{2,1,0:T(8,128)(2,1)S(1)} %convert_element_type.27), channel_id=1, source_target_pairs={{0,1},{1,0},{2,3},{3,2},{4,5},{5,4},{6,7},{7,6},{8,9},{9,8},{10,11... | collective-permute-start | bytes 294920 | tf_op jit(solution)/shard_map/ppermute | solution.py:160
  38.0 2.9 %collective-permute-start.11 = (f16[96,128]{1,0:T(8,128)(2,1)S(1)}, f16[96,128]{1,0:T(8,128)(2,1)S(1)}, u32[]{:S(2)}, u32[]{:S(2)}) collective-permute-start(f16[96,128]{1,0:T(8,128)(2,1)S(1)} %get-tuple-element.48), channel_id=1, source_target_pairs={{0,1},{1,0},{2,3},{3,2},{4,5},{5,4},{6,7},{7,6},{8,9},{9,8},{10,11... | collective-permute-start | bytes 73736 | tf_op jit(solution)/shard_map/ppermute | solution.py:160
  38.2 5.2 %collective-permute-start.12 = (f16[96,128]{1,0:T(8,128)(2,1)S(1)}, f16[96,128]{1,0:T(8,128)(2,1)S(1)}, u32[]{:S(2)}, u32[]{:S(2)}) collective-permute-start(f16[96,128]{1,0:T(8,128)(2,1)S(1)} %get-tuple-element.48), channel_id=1, source_target_pairs={{0,8},{1,9},{2,10},{3,11},{4,12},{5,13},{6,14},{7,15},{8,0},{9,1},... | collective-permute-start | bytes 73736 | tf_op jit(solution)/shard_map/ppermute | solution.py:160
  38.3 5.1 %collective-permute-start.13 = (f16[96,128]{1,0:T(8,128)(2,1)S(1)}, f16[96,128]{1,0:T(8,128)(2,1)S(1)}, u32[]{:S(2)}, u32[]{:S(2)}) collective-permute-start(f16[96,128]{1,0:T(8,128)(2,1)S(1)} %get-tuple-element.48), channel_id=1, source_target_pairs={{0,9},{1,8},{2,11},{3,10},{4,13},{5,12},{6,15},{7,14},{8,1},{9,0},... | collective-permute-start | bytes 73736 | tf_op jit(solution)/shard_map/ppermute | solution.py:160
  43.4 5.1 %collective-permute-start.14 = (f16[192,128]{1,0:T(8,128)(2,1)S(1)}, f16[192,128]{1,0:T(8,128)(2,1)S(1)}, u32[]{:S(2)}, u32[]{:S(2)}) collective-permute-start(f16[192,128]{1,0:T(8,128)(2,1)S(1)} %get-tuple-element.62), channel_id=1, source_target_pairs={{0,6},{1,7},{2,4},{3,5},{4,2},{5,3},{6,0},{7,1},{8,14},{9,15},{10,... | collective-permute-start | bytes 147464 | tf_op jit(solution)/shard_map/ppermute | solution.py:160
  45.8 4.1 %collective-permute-start.15 = (f16[192,128]{1,0:T(8,128)(2,1)S(1)}, f16[192,128]{1,0:T(8,128)(2,1)S(1)}, u32[]{:S(2)}, u32[]{:S(2)}) collective-permute-start(f16[192,128]{1,0:T(8,128)(2,1)S(1)} %get-tuple-element.61), channel_id=1, source_target_pairs={{0,4},{1,5},{2,6},{3,7},{4,0},{5,1},{6,2},{7,3},{8,12},{9,13},{10,... | collective-permute-start | bytes 147464 | tf_op jit(solution)/shard_map/ppermute | solution.py:160
  46.2 4.1 %collective-permute-start.16 = (f16[192,128]{1,0:T(8,128)(2,1)S(1)}, f16[192,128]{1,0:T(8,128)(2,1)S(1)}, u32[]{:S(2)}, u32[]{:S(2)}) collective-permute-start(f16[192,128]{1,0:T(8,128)(2,1)S(1)} %get-tuple-element.60), channel_id=1, source_target_pairs={{0,2},{1,3},{2,0},{3,1},{4,6},{5,7},{6,4},{7,5},{8,10},{9,11},{10,... | collective-permute-start | bytes 147464 | tf_op jit(solution)/shard_map/ppermute | solution.py:160

commit v5 on v4

--- a/solution.py
+++ b/solution.py
@@ -52,7 +52,7 @@
     given, before, refs = refs[:count], refs[count:][:carried], refs[count + carried :]
     keep_ref, send_ref, *refs = refs
     kept, refs = (refs[:count], refs[count:]) if fresh else (given, refs)
-    bands, own, slots, times, rates, semaphores, *bins = refs
+    bands, slots, times, rates, semaphores, *bins = refs
     fetches = [
         pltpu.make_async_copy(slot_ref, slots, semaphores.at[0]),
         pltpu.make_async_copy(time_ref, times, semaphores.at[1]),
@@ -60,9 +60,6 @@
     ]
     for fetch in fetches:
         fetch.start()
-    if fresh and sources[0] == 0:
-        copy = pltpu.make_async_copy(given[0], own, semaphores.at[3])
-        copy.start()
     chips = rates.shape[0] // 8
     together = len(bins)
     turns = bins[0].shape[0] // 4
@@ -81,9 +78,6 @@
         part[...] = jnp.zeros(part.shape, part.dtype)
     for index, relative in enumerate(sources):
         filtered, window_ref = kept[index], given[index]
-        if fresh and relative == 0:
-            copy.wait()
-            window_ref = own
         for number in range(images):
             if fresh:
                 low = rows * number // LANES * LANES
@@ -203,16 +197,14 @@
             ),
             out_shape=[shape((count // 2, rows, block), jnp.float32)] * 2 + [filtered] * (fresh * len(sources)),
             in_specs=[hbm, hbm, hbm, vmem]
-            + [hbm if x == 0 and fresh else vmem for x in sources]
-            + [vmem] * len(carried),
+            + [vmem] * (len(sources) + len(carried)),
             out_specs=[vmem] * (2 + fresh * len(sources)),
             scratch_shapes=[
                 pltpu.VMEM((4, 2 * LANES, 4 * LANES), jnp.bfloat16),
-                pltpu.VMEM((wide, lanes), jnp.bfloat16),
                 pltpu.SMEM(slot_epoch.shape, jnp.int32),
                 pltpu.SMEM(epoch_time.shape, jnp.int32),
                 pltpu.SMEM(rates.shape, jnp.int32),
-                pltpu.SemaphoreType.DMA((4,)),
+                pltpu.SemaphoreType.DMA((3,)),
             ]
             + [pltpu.VMEM((4 * count // together, reach + PACK, LANES), jnp.float32)] * together,
             compiler_params=pltpu.CompilerParams(vmem_limit_bytes=32 * 1024 * 1024),

time: 51.3 us -> 51.3 us (level)
  no operation moved by 1% of the time
where the time goes in v5:
time: 51.3 us; the launch traced here: 51.1 us
  starting transfers between devices  20.3 us (40%)
  waiting for transfers between devices  14 us (27%)
  Pallas kernels  13.7 us (27%)
  local copies, waits for them, and re-layouts  1.75 us (3%)
  between operations  0.79 us (2%)
  other arithmetic  0.58 us (1%)
    ppermute x17, starting transfers between devices, swap(): return lax.ppermute(array, 'vel', [(i, i ^ bits) for i in range(axis_size)])  20.3 us
    ppermute x17, waiting for transfers between devices, swap(): return lax.ppermute(array, 'vel', [(i, i ^ bits) for i in range(axis_size)])  14 us
    pallas_call x3, Pallas kernels, stack(): pl.pallas_call(functools.partial(stack_kernel, *(block, rows, sources, pe...  10.9 us
    pallas_call x1, Pallas kernels, local(): pl.pallas_call(functools.partial(window_kernel, block), out_shape=[shape(...  2.78 us
  transfers between devices with their start and end apart: 17, of which 10 were waited for; matrix products, arithmetic and copies ran while one was open for 1% of the time, Pallas kernels for 22%

profile of v5, /device:TPU:0, one launch (start us, length us, event | category | flops | bytes accessed | tf_op | source)
XLA Modules:
  0.0 51.1 jit_solution(15889430297443608743)
XLA Ops:
  0.6 3.0 %collective-permute-start = (s32[2]{0:T(128)}, s32[2]{0:T(128)S(1)}, u32[]{:S(2)}, u32[]{:S(2)}) collective-permute-start(s32[2]{0:T(128)} %bitcast.12), channel_id=1, source_target_pairs={{0,2},{1,3},{2,0},{3,1},{4,6},{5,7},{6,4},{7,5},{8,10},{9,11},{10,... | collective-permute-start | bytes 32 | tf_op jit(solution)/shard_map/ppermute | solution.py:154
  3.7 1.6 %collective-permute-start.1 = (s32[2]{0:T(128)}, s32[2]{0:T(128)S(1)}, u32[]{:S(2)}, u32[]{:S(2)}) collective-permute-start(s32[2]{0:T(128)} %bitcast.13), channel_id=1, source_target_pairs={{0,4},{1,5},{2,6},{3,7},{4,0},{5,1},{6,2},{7,3},{8,12},{9,13},{10,... | collective-permute-start | bytes 32 | tf_op jit(solution)/shard_map/ppermute | solution.py:154
  5.2 0.0 collective-permute-start.2
  5.2 0.0 copy-start.4
  5.2 0.0 copy-start
  5.2 0.0 copy-start.1
  5.3 0.0 copy-start.2
  5.3 2.8 %windows.1 = (bf16[176,768]{1,0:T(8,128)(2,1)}, bf16[176,768]{1,0:T(8,128)(2,1)}, bf16[176,768]{1,0:T(8,128)(2,1)}, bf16[176,768]{1,0:T(8,128)(2,1)}) custom-call(bf16[768,512]{1,0:T(8,128)(2,1)} %bitcast.16), custom_call_target="tpu_custom_call" | custom-call | flops 3000000000 | bytes 9000000 | tf_op jit(solution)/shard_map/windows/pallas_call | solution.py:169
  8.0 1.9 %collective-permute-start.6 = (bf16[176,768]{1,0:T(8,128)(2,1)}, bf16[176,768]{1,0:T(8,128)(2,1)S(1)}, u32[]{:S(2)}, u32[]{:S(2)}) collective-permute-start(bf16[176,768]{1,0:T(8,128)(2,1)} %get-tuple-element.30), channel_id=1, source_target_pairs={{0,2},{1,3},{2,0},{3,1},{4,6},{5,7},{6,4},{7,5},{8,10},{9,11},{10,... | collective-permute-start | bytes 811016 | tf_op jit(solution)/shard_map/ppermute | solution.py:154
  9.9 0.0 collective-permute-done
  9.9 0.0 collective-permute-done.1
  10.0 0.0 collective-permute-done.2
  10.0 0.0 copy-done.4
  10.0 0.1 pad_add_fusion
  10.0 1.6 %collective-permute-start.7 = (bf16[176,768]{1,0:T(8,128)(2,1)}, bf16[176,768]{1,0:T(8,128)(2,1)S(1)}, u32[]{:S(2)}, u32[]{:S(2)}) collective-permute-start(bf16[176,768]{1,0:T(8,128)(2,1)} %get-tuple-element.31), channel_id=1, source_target_pairs={{0,4},{1,5},{2,6},{3,7},{4,0},{5,1},{6,2},{7,3},{8,12},{9,13},{10,... | collective-permute-start | bytes 811016 | tf_op jit(solution)/shard_map/ppermute | solution.py:154
  11.6 0.0 collective-permute-start.3
  11.6 1.1 %collective-permute-done.3 = s32[8]{0:T(128)S(1)} collective-permute-done((s32[8]{0:T(128)S(1)}, s32[8]{0:T(128)S(1)}, u32[]{:S(2)}, u32[]{:S(2)}) %collective-permute-start.3) | collective-permute-done | bytes 64 | tf_op jit(solution)/shard_map/ppermute | solution.py:154
  12.8 0.1 pad_add_fusion.1
  12.8 2.6 %collective-permute-start.4 = (s32[16]{0:T(128)S(1)}, s32[16]{0:T(128)S(1)}, u32[]{:S(2)}, u32[]{:S(2)}) collective-permute-start(s32[16]{0:T(128)S(1)} %pad_add_fusion.1), channel_id=1, source_target_pairs={{0,8},{1,9},{2,10},{3,11},{4,12},{5,13},{6,14},{7,15},{8,0},{9,1},... | collective-permute-start | bytes 200 | tf_op jit(solution)/shard_map/ppermute | solution.py:154
  15.4 0.4 collective-permute-start.5
  15.8 1.5 %collective-permute-done.4 = s32[16]{0:T(128)S(1)} collective-permute-done((s32[16]{0:T(128)S(1)}, s32[16]{0:T(128)S(1)}, u32[]{:S(2)}, u32[]{:S(2)}) %collective-permute-start.4) | collective-permute-done | bytes 96 | tf_op jit(solution)/shard_map/ppermute | solution.py:154
  17.3 0.1 pad_add_fusion.2.rate_ref
  17.4 0.0 collective-permute-done.6.refs_1_
  17.4 0.0 collective-permute-done.7.refs_2_
  17.4 0.0 copy-done
  17.4 0.0 copy-done.1
  17.4 0.0 copy-done.2
  17.4 0.0 copy-start.3
  17.4 0.9 %copy-done.3 = bf16[176,768]{1,0:T(8,128)(2,1)S(1)} copy-done((bf16[176,768]{1,0:T(8,128)(2,1)S(1)}, bf16[176,768]{1,0:T(8,128)(2,1)}, u32[]{:S(2)}) %copy-start.3) | copy-done | bytes 270360
  18.3 4.5 %stack.3 = (f32[4,96,128]{2,1,0:T(8,128)S(1)}, f32[4,96,128]{2,1,0:T(8,128)S(1)}, bf16[8,4,192,128]{3,2,1,0:T(8,128)(2,1)S(1)}, bf16[8,4,192,128]{3,2,1,0:T(8,128)(2,1)S(1)}, bf16[8,4,192,128]{3,2,1,0:T(8,128)(2,1)S(1)}) custom-call(s32[64]{0:T(128)S(1)} %copy-done, s32[64]{0:T(128)S(1)} %copy-done.1, s32[32]{0:T(128)S(1)} %pad_add_fusion.2.rate_ref, ...), custom_call_target="tpu_custom_call" | custom-call | flops 5000000000 | bytes 15000000 | tf_op jit(solution)/shard_map/stack/pallas_call | solution.py:193
  22.8 2.0 %collective-permute-done.5.refs_0_ = bf16[176,768]{1,0:T(8,128)(2,1)S(1)} collective-permute-done((bf16[176,768]{1,0:T(8,128)(2,1)}, bf16[176,768]{1,0:T(8,128)(2,1)S(1)}, u32[]{:S(2)}, u32[]{:S(2)}) %collective-permute-start.5) | collective-permute-done | bytes 270368 | tf_op jit(solution)/shard_map/ppermute | solution.py:154
  24.9 2.3 %stack.4 = (f32[4,96,128]{2,1,0:T(8,128)S(1)}, f32[4,96,128]{2,1,0:T(8,128)S(1)}, bf16[8,4,192,128]{3,2,1,0:T(8,128)(2,1)S(1)}) custom-call(s32[64]{0:T(128)S(1)} %copy-done, s32[64]{0:T(128)S(1)} %copy-done.1, s32[32]{0:T(128)S(1)} %pad_add_fusion.2.rate_ref, bf16[96,512]{1,0:T(8,128)(2,1)S(1)} %copy-done.2, ...), custom_call_target="tpu_custom_call" | custom-call | flops 5000000000 | bytes 15000000 | tf_op jit(solution)/shard_map/stack/pallas_call | solution.py:193
  27.2 0.1 collective-permute-start.8
  27.2 1.3 %collective-permute-done.8 = f16[4,96,128]{2,1,0:T(8,128)(2,1)S(1)} collective-permute-done((f16[4,96,128]{2,1,0:T(8,128)(2,1)S(1)}, f16[4,96,128]{2,1,0:T(8,128)(2,1)S(1)}, u32[]{:S(2)}, u32[]{:S(2)}) %collective-permute-start.8) | collective-permute-done | bytes 98336 | tf_op jit(solution)/shard_map/ppermute | solution.py:154
  28.6 2.2 %collective-permute-start.9 = (f16[4,96,128]{2,1,0:T(8,128)(2,1)S(1)}, f16[4,96,128]{2,1,0:T(8,128)(2,1)S(1)}, u32[]{:S(2)}, u32[]{:S(2)}) collective-permute-start(f16[4,96,128]{2,1,0:T(8,128)(2,1)S(1)} %add_convert_fusion), channel_id=1, source_target_pairs={{0,8},{1,9},{2,10},{3,11},{4,12},{5,13},{6,14},{7,15},{8,0},{9,1},... | collective-permute-start | bytes 294920 | tf_op jit(solution)/shard_map/ppermute | solution.py:154
  30.7 4.2 %stack.5 = (f32[4,96,128]{2,1,0:T(8,128)S(1)}, f32[4,96,128]{2,1,0:T(8,128)S(1)}) custom-call(s32[64]{0:T(128)S(1)} %copy-done, s32[64]{0:T(128)S(1)} %copy-done.1, s32[32]{0:T(128)S(1)} %pad_add_fusion.2.rate_ref, bf16[96,512]{1,0:T(8,128)(2,1)S(1)} %copy-done.2, bf16[8,4,192,128]{3,2,1,0:T(8,128)(2,1)S(1)} %get-tuple-element.39.refs_0_, ...), custom_call_target="tpu_custom_call" | custom-call | flops 5000000000 | bytes 15000000 | tf_op jit(solution)/shard_map/stack/pallas_call | solution.py:193
  34.9 1.5 %collective-permute-done.9 = f16[4,96,128]{2,1,0:T(8,128)(2,1)S(1)} collective-permute-done((f16[4,96,128]{2,1,0:T(8,128)(2,1)S(1)}, f16[4,96,128]{2,1,0:T(8,128)(2,1)S(1)}, u32[]{:S(2)}, u32[]{:S(2)}) %collective-permute-start.9) | collective-permute-done | bytes 98336 | tf_op jit(solution)/shard_map/ppermute | solution.py:154
  36.5 0.1 collective-permute-start.10
  36.6 1.3 %collective-permute-done.10 = f16[4,96,128]{2,1,0:T(8,128)(2,1)S(1)} collective-permute-done((f16[4,96,128]{2,1,0:T(8,128)(2,1)S(1)}, f16[4,96,128]{2,1,0:T(8,128)(2,1)S(1)}, u32[]{:S(2)}, u32[]{:S(2)}) %collective-permute-start.10) | collective-permute-done | bytes 98336 | tf_op jit(solution)/shard_map/ppermute | solution.py:154
  37.9 0.1 fusion
  38.0 0.2 collective-permute-start.11
  38.2 0.1 collective-permute-start.12
  38.3 2.5 %collective-permute-start.13 = (f16[96,128]{1,0:T(8,128)(2,1)S(1)}, f16[96,128]{1,0:T(8,128)(2,1)S(1)}, u32[]{:S(2)}, u32[]{:S(2)}) collective-permute-start(f16[96,128]{1,0:T(8,128)(2,1)S(1)} %get-tuple-element.48), channel_id=1, source_target_pairs={{0,9},{1,8},{2,11},{3,10},{4,13},{5,12},{6,15},{7,14},{8,1},{9,0},... | collective-permute-start | bytes 73736 | tf_op jit(solution)/shard_map/ppermute | solution.py:154
  40.8 0.0 collective-permute-done.11
  40.8 2.5 %collective-permute-done.12 = f16[96,128]{1,0:T(8,128)(2,1)S(1)} collective-permute-done((f16[96,128]{1,0:T(8,128)(2,1)S(1)}, f16[96,128]{1,0:T(8,128)(2,1)S(1)}, u32[]{:S(2)}, u32[]{:S(2)}) %collective-permute-start.12) | collective-permute-done | bytes 24608 | tf_op jit(solution)/shard_map/ppermute | solution.py:154
  43.3 0.0 collective-permute-done.13
  43.4 2.4 %collective-permute-start.14 = (f16[192,128]{1,0:T(8,128)(2,1)S(1)}, f16[192,128]{1,0:T(8,128)(2,1)S(1)}, u32[]{:S(2)}, u32[]{:S(2)}) collective-permute-start(f16[192,128]{1,0:T(8,128)(2,1)S(1)} %get-tuple-element.62), channel_id=1, source_target_pairs={{0,6},{1,7},{2,4},{3,5},{4,2},{5,3},{6,0},{7,1},{8,14},{9,15},{10,... | collective-permute-start | bytes 147464 | tf_op jit(solution)/shard_map/ppermute | solution.py:154
  45.8 0.3 collective-permute-start.15
  46.1 1.4 %collective-permute-start.16 = (f16[192,128]{1,0:T(8,128)(2,1)S(1)}, f16[192,128]{1,0:T(8,128)(2,1)S(1)}, u32[]{:S(2)}, u32[]{:S(2)}) collective-permute-start(f16[192,128]{1,0:T(8,128)(2,1)S(1)} %get-tuple-element.60), channel_id=1, source_target_pairs={{0,2},{1,3},{2,0},{3,1},{4,6},{5,7},{6,4},{7,5},{8,10},{9,11},{10,... | collective-permute-start | bytes 147464 | tf_op jit(solution)/shard_map/ppermute | solution.py:154
  47.5 1.0 %collective-permute-done.14 = f16[192,128]{1,0:T(8,128)(2,1)S(1)} collective-permute-done((f16[192,128]{1,0:T(8,128)(2,1)S(1)}, f16[192,128]{1,0:T(8,128)(2,1)S(1)}, u32[]{:S(2)}, u32[]{:S(2)}) %collective-permute-start.14) | collective-permute-done | bytes 49184 | tf_op jit(solution)/shard_map/ppermute | solution.py:154
  48.5 1.4 %collective-permute-done.15 = f16[192,128]{1,0:T(8,128)(2,1)S(1)} collective-permute-done((f16[192,128]{1,0:T(8,128)(2,1)S(1)}, f16[192,128]{1,0:T(8,128)(2,1)S(1)}, u32[]{:S(2)}, u32[]{:S(2)}) %collective-permute-start.15) | collective-permute-done | bytes 49184 | tf_op jit(solution)/shard_map/ppermute | solution.py:154
  49.9 0.3 collective-permute-done.16
  50.2 0.1 broadcast_select_fusion.7
  50.3 0.1 convert_multiply_fusion
  50.4 0.8 %fusion.1 = (f32[96,512]{1,0:T(8,128)}, f32[1,96,512]{2,1,0:T(8,128)}) fusion(f32[192,512]{1,0:T(8,128)S(1)} %convert_multiply_fusion), kind=kLoop, calls=%fused_computation.26 | loop fusion | bytes 786432 | tf_op jit(solution)/shard_map/slice | solution.py:235
  (7 shorter events, 0.2 us)
Async XLA Ops:
  0.6 9.3 %collective-permute-start = (s32[2]{0:T(128)}, s32[2]{0:T(128)S(1)}, u32[]{:S(2)}, u32[]{:S(2)}) collective-permute-start(s32[2]{0:T(128)} %bitcast.12), channel_id=1, source_target_pairs={{0,2},{1,3},{2,0},{3,1},{4,6},{5,7},{6,4},{7,5},{8,10},{9,11},{10,... | collective-permute-start | bytes 32 | tf_op jit(solution)/shard_map/ppermute | solution.py:154
  3.7 6.3 %collective-permute-start.1 = (s32[2]{0:T(128)}, s32[2]{0:T(128)S(1)}, u32[]{:S(2)}, u32[]{:S(2)}) collective-permute-start(s32[2]{0:T(128)} %bitcast.13), channel_id=1, source_target_pairs={{0,4},{1,5},{2,6},{3,7},{4,0},{5,1},{6,2},{7,3},{8,12},{9,13},{10,... | collective-permute-start | bytes 32 | tf_op jit(solution)/shard_map/ppermute | solution.py:154
  5.2 4.7 %collective-permute-start.2 = (s32[2]{0:T(128)}, s32[2]{0:T(128)S(1)}, u32[]{:S(2)}, u32[]{:S(2)}) collective-permute-start(s32[2]{0:T(128)} %bitcast.14), channel_id=1, source_target_pairs={{0,6},{1,7},{2,4},{3,5},{4,2},{5,3},{6,0},{7,1},{8,14},{9,15},{10,... | collective-permute-start | bytes 32 | tf_op jit(solution)/shard_map/ppermute | solution.py:154
  5.2 4.7 %copy-start.4 = (s32[1,2]{1,0:T(1,128)S(1)}, s32[1,2]{1,0:T(1,128)}, u32[]{:S(2)}) copy-start(s32[1,2]{1,0:T(1,128)} %param.6) | copy-start | bytes 28
  5.2 12.1 %copy-start = (s32[64]{0:T(128)S(1)}, s32[64]{0:T(128)}, u32[]{:S(2)}) copy-start(s32[64]{0:T(128)} %slot_ref.5) | copy-start | bytes 772
  5.2 12.1 %copy-start.1 = (s32[64]{0:T(128)S(1)}, s32[64]{0:T(128)}, u32[]{:S(2)}) copy-start(s32[64]{0:T(128)} %time_ref.5) | copy-start | bytes 772
  5.3 12.1 %copy-start.2 = (bf16[96,512]{1,0:T(8,128)(2,1)S(1)}, bf16[96,512]{1,0:T(8,128)(2,1)}, u32[]{:S(2)}) copy-start(bf16[96,512]{1,0:T(8,128)(2,1)} %constant.44.clone.filter_ref) | copy-start | bytes 294916
  8.0 9.3 %collective-permute-start.6 = (bf16[176,768]{1,0:T(8,128)(2,1)}, bf16[176,768]{1,0:T(8,128)(2,1)S(1)}, u32[]{:S(2)}, u32[]{:S(2)}) collective-permute-start(bf16[176,768]{1,0:T(8,128)(2,1)} %get-tuple-element.30), channel_id=1, source_target_pairs={{0,2},{1,3},{2,0},{3,1},{4,6},{5,7},{6,4},{7,5},{8,10},{9,11},{10,... | collective-permute-start | bytes 811016 | tf_op jit(solution)/shard_map/ppermute | solution.py:154
  10.0 7.3 %collective-permute-start.7 = (bf16[176,768]{1,0:T(8,128)(2,1)}, bf16[176,768]{1,0:T(8,128)(2,1)S(1)}, u32[]{:S(2)}, u32[]{:S(2)}) collective-permute-start(bf16[176,768]{1,0:T(8,128)(2,1)} %get-tuple-element.31), channel_id=1, source_target_pairs={{0,4},{1,5},{2,6},{3,7},{4,0},{5,1},{6,2},{7,3},{8,12},{9,13},{10,... | collective-permute-start | bytes 811016 | tf_op jit(solution)/shard_map/ppermute | solution.py:154
  11.6 1.1 %collective-permute-start.3 = (s32[8]{0:T(128)S(1)}, s32[8]{0:T(128)S(1)}, u32[]{:S(2)}, u32[]{:S(2)}) collective-permute-start(s32[8]{0:T(128)S(1)} %pad_add_fusion), channel_id=1, source_target_pairs={{0,1},{1,0},{2,3},{3,2},{4,5},{5,4},{6,7},{7,6},{8,9},{9,8},{10,11... | collective-permute-start | bytes 104 | tf_op jit(solution)/shard_map/ppermute | solution.py:154
  12.8 4.4 %collective-permute-start.4 = (s32[16]{0:T(128)S(1)}, s32[16]{0:T(128)S(1)}, u32[]{:S(2)}, u32[]{:S(2)}) collective-permute-start(s32[16]{0:T(128)S(1)} %pad_add_fusion.1), channel_id=1, source_target_pairs={{0,8},{1,9},{2,10},{3,11},{4,12},{5,13},{6,14},{7,15},{8,0},{9,1},... | collective-permute-start | bytes 200 | tf_op jit(solution)/shard_map/ppermute | solution.py:154
  15.4 9.4 %collective-permute-start.5 = (bf16[176,768]{1,0:T(8,128)(2,1)}, bf16[176,768]{1,0:T(8,128)(2,1)S(1)}, u32[]{:S(2)}, u32[]{:S(2)}) collective-permute-start(bf16[176,768]{1,0:T(8,128)(2,1)} %get-tuple-element.28), channel_id=1, source_target_pairs={{0,6},{1,7},{2,4},{3,5},{4,2},{5,3},{6,0},{7,1},{8,14},{9,15},{10,... | collective-permute-start | bytes 811016 | tf_op jit(solution)/shard_map/ppermute | solution.py:154
  17.4 1.0 %copy-start.3 = (bf16[176,768]{1,0:T(8,128)(2,1)S(1)}, bf16[176,768]{1,0:T(8,128)(2,1)}, u32[]{:S(2)}) copy-start(bf16[176,768]{1,0:T(8,128)(2,1)} %get-tuple-element.29.refs_0_) | copy-start | bytes 811012
  27.2 1.4 %collective-permute-start.8 = (f16[4,96,128]{2,1,0:T(8,128)(2,1)S(1)}, f16[4,96,128]{2,1,0:T(8,128)(2,1)S(1)}, u32[]{:S(2)}, u32[]{:S(2)}) collective-permute-start(f16[4,96,128]{2,1,0:T(8,128)(2,1)S(1)} %convert_element_type.24), channel_id=1, source_target_pairs={{0,1},{1,0},{2,3},{3,2},{4,5},{5,4},{6,7},{7,6},{8,9},{9,8},{10,11... | collective-permute-start | bytes 294920 | tf_op jit(solution)/shard_map/ppermute | solution.py:154
  28.6 7.9 %collective-permute-start.9 = (f16[4,96,128]{2,1,0:T(8,128)(2,1)S(1)}, f16[4,96,128]{2,1,0:T(8,128)(2,1)S(1)}, u32[]{:S(2)}, u32[]{:S(2)}) collective-permute-start(f16[4,96,128]{2,1,0:T(8,128)(2,1)S(1)} %add_convert_fusion), channel_id=1, source_target_pairs={{0,8},{1,9},{2,10},{3,11},{4,12},{5,13},{6,14},{7,15},{8,0},{9,1},... | collective-permute-start | bytes 294920 | tf_op jit(solution)/shard_map/ppermute | solution.py:154
  36.5 1.4 %collective-permute-start.10 = (f16[4,96,128]{2,1,0:T(8,128)(2,1)S(1)}, f16[4,96,128]{2,1,0:T(8,128)(2,1)S(1)}, u32[]{:S(2)}, u32[]{:S(2)}) collective-permute-start(f16[4,96,128]{2,1,0:T(8,128)(2,1)S(1)} %convert_element_type.27), channel_id=1, source_target_pairs={{0,1},{1,0},{2,3},{3,2},{4,5},{5,4},{6,7},{7,6},{8,9},{9,8},{10,11... | collective-permute-start | bytes 294920 | tf_op jit(solution)/shard_map/ppermute | solution.py:154
  38.0 2.9 %collective-permute-start.11 = (f16[96,128]{1,0:T(8,128)(2,1)S(1)}, f16[96,128]{1,0:T(8,128)(2,1)S(1)}, u32[]{:S(2)}, u32[]{:S(2)}) collective-permute-start(f16[96,128]{1,0:T(8,128)(2,1)S(1)} %get-tuple-element.48), channel_id=1, source_target_pairs={{0,1},{1,0},{2,3},{3,2},{4,5},{5,4},{6,7},{7,6},{8,9},{9,8},{10,11... | collective-permute-start | bytes 73736 | tf_op jit(solution)/shard_map/ppermute | solution.py:154
  38.2 5.2 %collective-permute-start.12 = (f16[96,128]{1,0:T(8,128)(2,1)S(1)}, f16[96,128]{1,0:T(8,128)(2,1)S(1)}, u32[]{:S(2)}, u32[]{:S(2)}) collective-permute-start(f16[96,128]{1,0:T(8,128)(2,1)S(1)} %get-tuple-element.48), channel_id=1, source_target_pairs={{0,8},{1,9},{2,10},{3,11},{4,12},{5,13},{6,14},{7,15},{8,0},{9,1},... | collective-permute-start | bytes 73736 | tf_op jit(solution)/shard_map/ppermute | solution.py:154
  38.3 5.1 %collective-permute-start.13 = (f16[96,128]{1,0:T(8,128)(2,1)S(1)}, f16[96,128]{1,0:T(8,128)(2,1)S(1)}, u32[]{:S(2)}, u32[]{:S(2)}) collective-permute-start(f16[96,128]{1,0:T(8,128)(2,1)S(1)} %get-tuple-element.48), channel_id=1, source_target_pairs={{0,9},{1,8},{2,11},{3,10},{4,13},{5,12},{6,15},{7,14},{8,1},{9,0},... | collective-permute-start | bytes 73736 | tf_op jit(solution)/shard_map/ppermute | solution.py:154
  43.4 5.1 %collective-permute-start.14 = (f16[192,128]{1,0:T(8,128)(2,1)S(1)}, f16[192,128]{1,0:T(8,128)(2,1)S(1)}, u32[]{:S(2)}, u32[]{:S(2)}) collective-permute-start(f16[192,128]{1,0:T(8,128)(2,1)S(1)} %get-tuple-element.62), channel_id=1, source_target_pairs={{0,6},{1,7},{2,4},{3,5},{4,2},{5,3},{6,0},{7,1},{8,14},{9,15},{10,... | collective-permute-start | bytes 147464 | tf_op jit(solution)/shard_map/ppermute | solution.py:154
  45.8 4.1 %collective-permute-start.15 = (f16[192,128]{1,0:T(8,128)(2,1)S(1)}, f16[192,128]{1,0:T(8,128)(2,1)S(1)}, u32[]{:S(2)}, u32[]{:S(2)}) collective-permute-start(f16[192,128]{1,0:T(8,128)(2,1)S(1)} %get-tuple-element.61), channel_id=1, source_target_pairs={{0,4},{1,5},{2,6},{3,7},{4,0},{5,1},{6,2},{7,3},{8,12},{9,13},{10,... | collective-permute-start | bytes 147464 | tf_op jit(solution)/shard_map/ppermute | solution.py:154
  46.1 4.1 %collective-permute-start.16 = (f16[192,128]{1,0:T(8,128)(2,1)S(1)}, f16[192,128]{1,0:T(8,128)(2,1)S(1)}, u32[]{:S(2)}, u32[]{:S(2)}) collective-permute-start(f16[192,128]{1,0:T(8,128)(2,1)S(1)} %get-tuple-element.60), channel_id=1, source_target_pairs={{0,2},{1,3},{2,0},{3,1},{4,6},{5,7},{6,4},{7,5},{8,10},{9,11},{10,... | collective-permute-start | bytes 147464 | tf_op jit(solution)/shard_map/ppermute | solution.py:154
